TPU v7x, 256 devices: a whole 4x4x8 slice. The times are simulated.
256 devices in a mesh: row: 16 (over z_lo, x), col: 16 (over y, z_hi, core).
Axes of the slice: x: 4, y: 4, z: 8 (z_hi: 2, z_lo: 4; z = z_hi * 4 + z_lo), core: 2. Of those that a mesh axis runs over, the one named last changes fastest.
Arguments:
- tokens: bfloat16 [256, 8192], P('row', 'col'), may hold values from -6 to 6
- gate_weight: bfloat16 [8192, 26624], P('col', 'row'), may hold values from -0.0625 to 0.0625
- up_weight: bfloat16 [8192, 26624], P('col', 'row'), may hold values from -0.0625 to 0.0625
- down_weight: bfloat16 [26624, 8192], P('row', 'col'), may hold values from -0.0390625 to 0.0390625
- out_grad: bfloat16 [256, 8192], P('row', 'col'), may hold values from -6 to 6
Outputs:
- input_grad: bfloat16 [256, 8192], P('row', 'col')
- gate_grad: bfloat16 [8192, 26624], P('col', 'row')
- up_grad: bfloat16 [8192, 26624], P('col', 'row')
- down_grad: bfloat16 [26624, 8192], P('row', 'col')
All inputs are finite; a program needn't handle non-finite values.
Results may differ from a plain program's by a relative error of at most 0.005.
Values may be sent and summed in bfloat16 or wider, within the bound.
No kernel may reach another device: no remote copies, remote signals or barrier semaphores. Data moves between devices by JAX's collectives and lax.ppermute only.
A program may use at most 64 MiB of HBM per device.

v0:
```python
import jax
import jax.numpy as jnp
from jax import lax
from jax.sharding import PartitionSpec as P

F32 = jnp.float32
BF16 = jnp.bfloat16


def swapped(axis, mask):
    return lambda a: lax.ppermute(a, axis, [(i, i ^ mask) for i in range(16)])


def on_x(k):
    return swapped("row", k)


def on_z_lo(k):
    return swapped("row", 4 * k)


def on_y(k):
    return swapped("col", 4 * k)


on_z_hi = swapped("col", 2)
on_core = swapped("col", 1)

def xor_blocks(a, place):
    for bit, size in ((4, 32), (2, 16), (1, 8)):
        parts = a.reshape(-1, 2, size, a.shape[1])
        other = jnp.stack((parts[:, 1], parts[:, 0]), axis=1)
        a = jnp.where((place & bit) > 0, other, parts).reshape(a.shape)
    return a


def pointwise(gate, up, hidden_cot):
    sigma = jax.nn.sigmoid(gate)
    silu = gate * sigma
    hidden = (silu * up).astype(BF16)
    up_cot = (hidden_cot * silu).astype(BF16)
    gate_cot = (hidden_cot * up * sigma * (1.0 + gate * (1.0 - sigma))).astype(BF16)
    return jnp.concatenate((hidden, gate_cot, up_cot), axis=-1)


def dot(left, right, dims):
    return lax.dot_general(left, right, (dims, ((), ())), preferred_element_type=F32)


def side_by_side(left, right):
    n = left.shape[1]
    zero = jnp.zeros((), left.dtype)
    return lax.pad(left, zero, ((0, 0, 0), (0, n, 0))) + lax.pad(right, zero, ((0, 0, 0), (n, 0, 0)))


def after(value, other):
    return lax.optimization_barrier((value, other))[0]


def body(tokens, gate_weight, up_weight, down_weight, out_grad):
    width = gate_weight.shape[1]
    depth = tokens.shape[1]
    col = lax.axis_index("col")
    place = (col % 2) * 4 + col // 4

    both = side_by_side(tokens, out_grad)
    own = jnp.concatenate([both] + [on_z_lo(k)(both) for k in (3, 2, 1)], axis=0)
    own = xor_blocks(own, place)
    near, far = on_x(2)(own), [on_x(1)(own), on_x(3)(own)]

    def partial_sums(chunk):
        token, cot = chunk[:, :depth], chunk[:, depth:]
        return jnp.concatenate(
            (
                dot(token, gate_weight, ((1,), (0,))),
                dot(token, up_weight, ((1,), (0,))),
                dot(cot, down_weight, ((1,), (1,))),
            ),
            axis=1,
        ).reshape(-1, 64, 3 * width)

    def reduced_on_core(part):
        return part[:, :32] + on_core(part[:, 32:])

    def sent_on_y(pair):
        return [pair[:, 8 * q : 8 * q + 8].astype(BF16) for q in (3, 2, 1)]

    def reduced_on_y(pair, others):
        total = pair[:, :8]
        for other in others:
            total = total + other.astype(F32)
        return total

    def local(total, other):
        total = total + other.astype(F32)
        return pointwise(total[..., :width], total[..., width : 2 * width], total[..., 2 * width :])

    def joined(half, other):
        return jnp.concatenate((half, other), axis=1).reshape(128, 3 * width)

    def input_part(full):
        return dot(full[:, width : 2 * width], gate_weight, ((1,), (1,))) + dot(
            full[:, 2 * width :], up_weight, ((1,), (1,))
        )

    part = partial_sums(own)
    near = after(near, part)
    part = jnp.concatenate((part, partial_sums(near)), axis=0)
    far = jnp.concatenate(after(far, part), axis=0)
    pairs = [reduced_on_core(part), reduced_on_core(partial_sums(far))]
    sent = [sent_on_y(pair) for pair in pairs]
    others = [[on_y(q)(block) for q, block in zip((3, 2, 1), blocks)] for blocks in sent]
    totals = [
        reduced_on_y(pairs[0], after(others[0], sent[1])),
        reduced_on_y(pairs[1], others[1]),
    ]
    sent = [total.astype(BF16) for total in totals]
    others = [on_z_hi(total) for total in sent]
    first = local(totals[0], after(others[0], sent[1]))
    second = local(totals[1], others[1])
    others = [
        after([on_y(q)(first) for q in (1, 2, 3)], second),
        after([on_y(q)(second) for q in (3, 2, 1)], first)[::-1],
    ]
    halves = [jnp.concatenate([a] + b, axis=1) for a, b in zip((first, second), others)]
    others = [on_core(half) for half in halves]
    fulls = [joined(halves[0], others[0])]
    back = input_part(fulls[0])
    back, sent = back[:64], back[64:]
    fulls.append(joined(halves[1], after(others[1], sent)))
    back_total = back + on_x(2)(sent)
    back = input_part(fulls[1])
    back_total = back_total + on_x(3)(back[64:]) + on_x(1)(back[:64])
    back_total = xor_blocks(back_total, place)
    total = back_total[:16]
    for i, k in enumerate((3, 2, 1)):
        total = total + on_z_lo(k)(back_total[16 * i + 16 : 16 * i + 32])
    input_grad = total.astype(BF16)

    panel = jnp.concatenate((own, near, far), axis=0)
    cots = after(jnp.concatenate(fulls, axis=0), back)
    factor = F32(panel.shape[0]) ** (-0.5)
    token, cot = panel[:, :depth], panel[:, depth:]
    rows = ((0,), (0,))
    down_grad = (dot(cots[:, :width], cot, rows) * factor).astype(BF16)
    gate_grad = (dot(token, cots[:, width : 2 * width], rows) * factor).astype(BF16)
    up_grad = (dot(token, cots[:, 2 * width :], rows) * factor).astype(BF16)
    return (input_grad, gate_grad, up_grad, down_grad)


def solution(mesh):
    in_specs = (P("row", "col"), P("col", "row"), P("col", "row"), P("row", "col"), P("row", "col"))
    out_specs = (P("row", "col"), P("col", "row"), P("col", "row"), P("row", "col"))
    return jax.shard_map(body, mesh=mesh, in_specs=in_specs, out_specs=out_specs, check_vma=False)
```

profile of v0, /device:TPU:24, one launch (start us, length us, event | category | flops | bytes accessed | tf_op | source)
XLA Modules:
  0.0 87.6 jit_solution(4044167991153106145)
XLA Ops:
  0.6 0.9 pad_add_fusion
  1.5 4.6 %collective-permute-start = (bf16[16,1024]{1,0:T(8,128)(2,1)S(1)}, bf16[16,1024]{1,0:T(8,128)(2,1)S(1)}, u32[]{:S(2)}, u32[]{:S(2)}) collective-permute-start(bf16[16,1024]{1,0:T(8,128)(2,1)S(1)} %pad_add_fusion), channel_id=1, source_target_pairs={{0,192},{16,208},{32,224},{48,240},{64,128},{80,144},{96,160},{112... | collective-permute-start | bytes 98312 | tf_op jit(solution)/shard_map/ppermute | solution.py:11
  6.7 1.5 %collective-permute-done = bf16[16,1024]{1,0:T(8,128)(2,1)S(1)} collective-permute-done((bf16[16,1024]{1,0:T(8,128)(2,1)S(1)}, bf16[16,1024]{1,0:T(8,128)(2,1)S(1)}, u32[]{:S(2)}, u32[]{:S(2)}) %collective-permute-start) | collective-permute-done | bytes 32800 | tf_op jit(solution)/shard_map/ppermute | solution.py:11
  8.2 2.7 %collective-permute-done.1 = bf16[16,1024]{1,0:T(8,128)(2,1)S(1)} collective-permute-done((bf16[16,1024]{1,0:T(8,128)(2,1)S(1)}, bf16[16,1024]{1,0:T(8,128)(2,1)S(1)}, u32[]{:S(2)}, u32[]{:S(2)}) %collective-permute-start.1) | collective-permute-done | bytes 32800 | tf_op jit(solution)/shard_map/ppermute | solution.py:11
  11.3 3.1 %collective-permute-start.3 = (bf16[64,1024]{1,0:T(8,128)(2,1)S(1)}, bf16[64,1024]{1,0:T(8,128)(2,1)S(1)}, u32[]{:S(2)}, u32[]{:S(2)}) collective-permute-start(bf16[64,1024]{1,0:T(8,128)(2,1)S(1)} %fusion.24), channel_id=1, source_target_pairs={{0,32},{16,48},{32,0},{48,16},{64,96},{80,112},{96,64},{112,80},{1... | collective-permute-start | bytes 393224 | tf_op jit(solution)/shard_map/ppermute | solution.py:11
  17.1 1.8 %collective-permute-done.3 = bf16[64,1024]{1,0:T(8,128)(2,1)S(1)} collective-permute-done((bf16[64,1024]{1,0:T(8,128)(2,1)S(1)}, bf16[64,1024]{1,0:T(8,128)(2,1)S(1)}, u32[]{:S(2)}, u32[]{:S(2)}) %collective-permute-start.3) | collective-permute-done | bytes 131104 | tf_op jit(solution)/shard_map/ppermute | solution.py:11
  21.2 0.7 fusion.21
  24.2 2.6 %collective-permute-start.6 = (bf16[2,8,4992]{2,1,0:T(8,128)(2,1)S(1)}, bf16[2,8,4992]{2,1,0:T(8,128)(2,1)S(1)}, u32[]{:S(2)}, u32[]{:S(2)}) collective-permute-start(bf16[2,8,4992]{2,1,0:T(8,128)(2,1)S(1)} %get-tuple-element.39), channel_id=1, source_target_pairs={{0,8},{1,9},{2,10},{3,11},{4,12},{5,13},{6,14},{7,15},{8,0},{9,1},... | collective-permute-start | bytes 479240 | tf_op jit(solution)/shard_map/ppermute | solution.py:11
  26.8 1.3 %collective-permute-start.7 = (bf16[2,8,4992]{2,1,0:T(8,128)(2,1)S(1)}, bf16[2,8,4992]{2,1,0:T(8,128)(2,1)S(1)}, u32[]{:S(2)}, u32[]{:S(2)}) collective-permute-start(bf16[2,8,4992]{2,1,0:T(8,128)(2,1)S(1)} %get-tuple-element.38), channel_id=1, source_target_pairs={{0,4},{1,5},{2,6},{3,7},{4,0},{5,1},{6,2},{7,3},{8,12},{9,13},{10,... | collective-permute-start | bytes 479240 | tf_op jit(solution)/shard_map/ppermute | solution.py:11
  28.6 2.6 %collective-permute-start.13 = (bf16[2,8,4992]{2,1,0:T(8,128)(2,1)S(1)}, bf16[2,8,4992]{2,1,0:T(8,128)(2,1)S(1)}, u32[]{:S(2)}, u32[]{:S(2)}) collective-permute-start(bf16[2,8,4992]{2,1,0:T(8,128)(2,1)S(1)} %get-tuple-element.43), channel_id=1, source_target_pairs={{0,8},{1,9},{2,10},{3,11},{4,12},{5,13},{6,14},{7,15},{8,0},{9,1},... | collective-permute-start | bytes 479240 | tf_op jit(solution)/shard_map/ppermute | solution.py:11
  31.2 5.0 %collective-permute-done.5 = bf16[2,8,4992]{2,1,0:T(8,128)(2,1)S(1)} collective-permute-done((bf16[2,8,4992]{2,1,0:T(8,128)(2,1)S(1)}, bf16[2,8,4992]{2,1,0:T(8,128)(2,1)S(1)}, u32[]{:S(2)}, u32[]{:S(2)}) %collective-permute-start.5) | collective-permute-done | bytes 159776 | tf_op jit(solution)/shard_map/ppermute | solution.py:11
  36.6 5.1 %collective-permute-start.11 = (bf16[2,8,4992]{2,1,0:T(8,128)(2,1)S(1)}, bf16[2,8,4992]{2,1,0:T(8,128)(2,1)S(1)}, u32[]{:S(2)}, u32[]{:S(2)}) collective-permute-start(bf16[2,8,4992]{2,1,0:T(8,128)(2,1)S(1)} %fusion.47), channel_id=1, source_target_pairs={{0,2},{1,3},{2,0},{3,1},{4,6},{5,7},{6,4},{7,5},{8,10},{9,11},{10,... | collective-permute-start | bytes 479240 | tf_op jit(solution)/shard_map/ppermute | solution.py:11
  42.4 4.9 %collective-permute-start.18 = (bf16[2,8,4992]{2,1,0:T(8,128)(2,1)S(1)}, bf16[2,8,4992]{2,1,0:T(8,128)(2,1)S(1)}, u32[]{:S(2)}, u32[]{:S(2)}) collective-permute-start(bf16[2,8,4992]{2,1,0:T(8,128)(2,1)S(1)} %fusion.48), channel_id=1, source_target_pairs={{0,2},{1,3},{2,0},{3,1},{4,6},{5,7},{6,4},{7,5},{8,10},{9,11},{10,... | collective-permute-start | bytes 479240 | tf_op jit(solution)/shard_map/ppermute | solution.py:11
  47.8 4.0 %collective-permute-start.15 = (bf16[2,8,4992]{2,1,0:T(8,128)(2,1)S(1)}, bf16[2,8,4992]{2,1,0:T(8,128)(2,1)S(1)}, u32[]{:S(2)}, u32[]{:S(2)}) collective-permute-start(bf16[2,8,4992]{2,1,0:T(8,128)(2,1)S(1)} %get-tuple-element.53), channel_id=1, source_target_pairs={{0,4},{1,5},{2,6},{3,7},{4,0},{5,1},{6,2},{7,3},{8,12},{9,13},{10,... | collective-permute-start | bytes 479240 | tf_op jit(solution)/shard_map/ppermute | solution.py:11
  51.7 2.8 %collective-permute-start.17 = (bf16[2,8,4992]{2,1,0:T(8,128)(2,1)S(1)}, bf16[2,8,4992]{2,1,0:T(8,128)(2,1)S(1)}, u32[]{:S(2)}, u32[]{:S(2)}) collective-permute-start(bf16[2,8,4992]{2,1,0:T(8,128)(2,1)S(1)} %get-tuple-element.53), channel_id=1, source_target_pairs={{0,12},{1,13},{2,14},{3,15},{4,8},{5,9},{6,10},{7,11},{8,4},{9,5},... | collective-permute-start | bytes 479240 | tf_op jit(solution)/shard_map/ppermute | solution.py:11
  54.5 1.1 %collective-permute-done.18 = bf16[2,8,4992]{2,1,0:T(8,128)(2,1)S(1)} collective-permute-done((bf16[2,8,4992]{2,1,0:T(8,128)(2,1)S(1)}, bf16[2,8,4992]{2,1,0:T(8,128)(2,1)S(1)}, u32[]{:S(2)}, u32[]{:S(2)}) %collective-permute-start.18) | collective-permute-done | bytes 159776 | tf_op jit(solution)/shard_map/ppermute | solution.py:11
  55.8 1.3 %collective-permute-start.21 = (bf16[2,8,4992]{2,1,0:T(8,128)(2,1)S(1)}, bf16[2,8,4992]{2,1,0:T(8,128)(2,1)S(1)}, u32[]{:S(2)}, u32[]{:S(2)}) collective-permute-start(bf16[2,8,4992]{2,1,0:T(8,128)(2,1)S(1)} %get-tuple-element.54), channel_id=1, source_target_pairs={{0,12},{1,13},{2,14},{3,15},{4,8},{5,9},{6,10},{7,11},{8,4},{9,5},... | collective-permute-start | bytes 479240 | tf_op jit(solution)/shard_map/ppermute | solution.py:11
  57.1 3.3 %collective-permute-start.22 = (bf16[2,8,4992]{2,1,0:T(8,128)(2,1)S(1)}, bf16[2,8,4992]{2,1,0:T(8,128)(2,1)S(1)}, u32[]{:S(2)}, u32[]{:S(2)}) collective-permute-start(bf16[2,8,4992]{2,1,0:T(8,128)(2,1)S(1)} %get-tuple-element.54), channel_id=1, source_target_pairs={{0,8},{1,9},{2,10},{3,11},{4,12},{5,13},{6,14},{7,15},{8,0},{9,1},... | collective-permute-start | bytes 479240 | tf_op jit(solution)/shard_map/ppermute | solution.py:11
  60.4 2.8 %collective-permute-done.17 = bf16[2,8,4992]{2,1,0:T(8,128)(2,1)S(1)} collective-permute-done((bf16[2,8,4992]{2,1,0:T(8,128)(2,1)S(1)}, bf16[2,8,4992]{2,1,0:T(8,128)(2,1)S(1)}, u32[]{:S(2)}, u32[]{:S(2)}) %collective-permute-start.17) | collective-permute-done | bytes 159776 | tf_op jit(solution)/shard_map/ppermute | solution.py:11
  63.4 3.3 %collective-permute-done.21 = bf16[2,8,4992]{2,1,0:T(8,128)(2,1)S(1)} collective-permute-done((bf16[2,8,4992]{2,1,0:T(8,128)(2,1)S(1)}, bf16[2,8,4992]{2,1,0:T(8,128)(2,1)S(1)}, u32[]{:S(2)}, u32[]{:S(2)}) %collective-permute-start.21) | collective-permute-done | bytes 159776 | tf_op jit(solution)/shard_map/ppermute | solution.py:11
  67.1 0.7 fusion.9
  67.8 0.7 convolution_add_fusion.1
  69.3 0.7 fusion.7
  70.0 2.8 %collective-permute-start.20 = (f32[64,512]{1,0:T(8,128)S(1)}, f32[64,512]{1,0:T(8,128)S(1)}, u32[]{:S(2)}, u32[]{:S(2)}) collective-permute-start(f32[64,512]{1,0:T(8,128)S(1)} %slice.267), channel_id=1, source_target_pairs={{0,32},{16,48},{32,0},{48,16},{64,96},{80,112},{96,64},{112,80},{1... | collective-permute-start | bytes 393224 | tf_op jit(solution)/shard_map/ppermute | solution.py:11
  72.8 0.7 convolution_add_fusion
  73.5 1.2 %collective-permute-start.25 = (f32[64,512]{1,0:T(8,128)S(1)}, f32[64,512]{1,0:T(8,128)S(1)}, u32[]{:S(2)}, u32[]{:S(2)}) collective-permute-start(f32[64,512]{1,0:T(8,128)S(1)} %get-tuple-element.50), channel_id=1, source_target_pairs={{0,48},{16,32},{32,16},{48,0},{64,112},{80,96},{96,80},{112,64},{1... | collective-permute-start | bytes 393224 | tf_op jit(solution)/shard_map/ppermute | solution.py:11
  74.7 1.8 %multiply_convert_fusion = bf16[1664,512]{1,0:T(8,128)(2,1)} fusion(bf16[256,4992]{1,0:T(8,128)(2,1)S(1)} %pad_maximum_fusion.2, bf16[256,1024]{1,0:T(8,128)(2,1)S(1)} %pad_maximum_fusion.5), kind=kOutput, calls=%fused_computation.5 | convolution fusion | flops 437911552 | bytes 2818048 | tf_op jit(solution)/shard_map/dot_general | solution.py:47
  76.5 1.9 %multiply_convert_fusion.1 = bf16[512,1664]{1,0:T(8,128)(2,1)} fusion(bf16[256,4992]{1,0:T(8,128)(2,1)S(1)} %pad_maximum_fusion.2, bf16[256,1024]{1,0:T(8,128)(2,1)S(1)} %pad_maximum_fusion.5), kind=kOutput, calls=%fused_computation.6 | convolution fusion | flops 437911552 | bytes 2818048 | tf_op jit(solution)/shard_map/dot_general | solution.py:47
  78.4 1.7 %collective-permute-done.25 = f32[64,512]{1,0:T(8,128)S(1)} collective-permute-done((f32[64,512]{1,0:T(8,128)S(1)}, f32[64,512]{1,0:T(8,128)S(1)}, u32[]{:S(2)}, u32[]{:S(2)}) %collective-permute-start.25) | collective-permute-done | bytes 131104 | tf_op jit(solution)/shard_map/ppermute | solution.py:11
  80.3 1.6 %collective-permute-start.27 = (f32[16,512]{1,0:T(8,128)S(1)}, f32[16,512]{1,0:T(8,128)S(1)}, u32[]{:S(2)}, u32[]{:S(2)}) collective-permute-start(f32[16,512]{1,0:T(8,128)S(1)} %get-tuple-element.56), channel_id=1, source_target_pairs={{0,192},{16,208},{32,224},{48,240},{64,128},{80,144},{96,160},{112... | collective-permute-start | bytes 98312 | tf_op jit(solution)/shard_map/ppermute | solution.py:11
  81.8 2.9 %collective-permute-start.29 = (f32[16,512]{1,0:T(8,128)S(1)}, f32[16,512]{1,0:T(8,128)S(1)}, u32[]{:S(2)}, u32[]{:S(2)}) collective-permute-start(f32[16,512]{1,0:T(8,128)S(1)} %get-tuple-element.57), channel_id=1, source_target_pairs={{0,64},{16,80},{32,96},{48,112},{64,0},{80,16},{96,32},{112,48},{1... | collective-permute-start | bytes 98312 | tf_op jit(solution)/shard_map/ppermute | solution.py:11
  84.7 1.9 %multiply_convert_fusion.2 = bf16[512,1664]{1,0:T(8,128)(2,1)} fusion(bf16[256,4992]{1,0:T(8,128)(2,1)S(1)} %pad_maximum_fusion.2, bf16[256,1024]{1,0:T(8,128)(2,1)S(1)} %pad_maximum_fusion.5), kind=kOutput, calls=%fused_computation.7 | convolution fusion | flops 437911552 | bytes 2818048 | tf_op jit(solution)/shard_map/dot_general | solution.py:47
  (103 shorter events, 12.7 us)
Async XLA Ops:
  0.6 16.0 %copy-start = (bf16[512,1664]{1,0:T(8,128)(2,1)S(1)}, bf16[512,1664]{1,0:T(8,128)(2,1)}, u32[]{:S(2)}) copy-start(bf16[512,1664]{1,0:T(8,128)(2,1)} %param.6) | copy-start | bytes 5111812
  1.5 6.7 %collective-permute-start = (bf16[16,1024]{1,0:T(8,128)(2,1)S(1)}, bf16[16,1024]{1,0:T(8,128)(2,1)S(1)}, u32[]{:S(2)}, u32[]{:S(2)}) collective-permute-start(bf16[16,1024]{1,0:T(8,128)(2,1)S(1)} %pad_add_fusion), channel_id=1, source_target_pairs={{0,192},{16,208},{32,224},{48,240},{64,128},{80,144},{96,160},{112... | collective-permute-start | bytes 98312 | tf_op jit(solution)/shard_map/ppermute | solution.py:11
  6.1 4.8 %collective-permute-start.1 = (bf16[16,1024]{1,0:T(8,128)(2,1)S(1)}, bf16[16,1024]{1,0:T(8,128)(2,1)S(1)}, u32[]{:S(2)}, u32[]{:S(2)}) collective-permute-start(bf16[16,1024]{1,0:T(8,128)(2,1)S(1)} %pad_add_fusion), channel_id=1, source_target_pairs={{0,128},{16,144},{32,160},{48,176},{64,192},{80,208},{96,224},{112... | collective-permute-start | bytes 98312 | tf_op jit(solution)/shard_map/ppermute | solution.py:11
  6.1 4.8 %collective-permute-start.2 = (bf16[16,1024]{1,0:T(8,128)(2,1)S(1)}, bf16[16,1024]{1,0:T(8,128)(2,1)S(1)}, u32[]{:S(2)}, u32[]{:S(2)}) collective-permute-start(bf16[16,1024]{1,0:T(8,128)(2,1)S(1)} %pad_add_fusion), channel_id=1, source_target_pairs={{0,64},{16,80},{32,96},{48,112},{64,0},{80,16},{96,32},{112,48},{1... | collective-permute-start | bytes 98312 | tf_op jit(solution)/shard_map/ppermute | solution.py:11
  11.1 5.0 %copy-start.1 = (bf16[512,1664]{1,0:T(8,128)(2,1)S(1)}, bf16[512,1664]{1,0:T(8,128)(2,1)}, u32[]{:S(2)}) copy-start(bf16[512,1664]{1,0:T(8,128)(2,1)} %param.7) | copy-start | bytes 5111812
  11.3 7.7 %collective-permute-start.3 = (bf16[64,1024]{1,0:T(8,128)(2,1)S(1)}, bf16[64,1024]{1,0:T(8,128)(2,1)S(1)}, u32[]{:S(2)}, u32[]{:S(2)}) collective-permute-start(bf16[64,1024]{1,0:T(8,128)(2,1)S(1)} %fusion.24), channel_id=1, source_target_pairs={{0,32},{16,48},{32,0},{48,16},{64,96},{80,112},{96,64},{112,80},{1... | collective-permute-start | bytes 393224 | tf_op jit(solution)/shard_map/ppermute | solution.py:11
  14.4 6.3 %collective-permute-start.8 = (bf16[64,1024]{1,0:T(8,128)(2,1)S(1)}, bf16[64,1024]{1,0:T(8,128)(2,1)S(1)}, u32[]{:S(2)}, u32[]{:S(2)}) collective-permute-start(bf16[64,1024]{1,0:T(8,128)(2,1)S(1)} %fusion.24), channel_id=1, source_target_pairs={{0,16},{16,0},{32,48},{48,32},{64,80},{80,64},{96,112},{112,96},{1... | collective-permute-start | bytes 393224 | tf_op jit(solution)/shard_map/ppermute | solution.py:11
  15.0 6.2 %collective-permute-start.9 = (bf16[64,1024]{1,0:T(8,128)(2,1)S(1)}, bf16[64,1024]{1,0:T(8,128)(2,1)S(1)}, u32[]{:S(2)}, u32[]{:S(2)}) collective-permute-start(bf16[64,1024]{1,0:T(8,128)(2,1)S(1)} %fusion.24), channel_id=1, source_target_pairs={{0,48},{16,32},{32,16},{48,0},{64,112},{80,96},{96,80},{112,64},{1... | collective-permute-start | bytes 393224 | tf_op jit(solution)/shard_map/ppermute | solution.py:11
  20.6 3.1 %collective-permute-start.4 = (f32[2,32,4992]{2,1,0:T(8,128)S(1)}, f32[2,32,4992]{2,1,0:T(8,128)S(1)}, u32[]{:S(2)}, u32[]{:S(2)}) collective-permute-start(f32[2,32,4992]{2,1,0:T(8,128)S(1)} %fusion.2), channel_id=1, source_target_pairs={{0,1},{1,0},{2,3},{3,2},{4,5},{5,4},{6,7},{7,6},{8,9},{9,8},{10,11... | collective-permute-start | bytes 3833864 | tf_op jit(solution)/shard_map/ppermute | solution.py:11
  23.0 5.1 %collective-permute-start.10 = (f32[2,32,4992]{2,1,0:T(8,128)S(1)}, f32[2,32,4992]{2,1,0:T(8,128)S(1)}, u32[]{:S(2)}, u32[]{:S(2)}) collective-permute-start(f32[2,32,4992]{2,1,0:T(8,128)S(1)} %slice.253), channel_id=1, source_target_pairs={{0,1},{1,0},{2,3},{3,2},{4,5},{5,4},{6,7},{7,6},{8,9},{9,8},{10,11... | collective-permute-start | bytes 3833864 | tf_op jit(solution)/shard_map/ppermute | solution.py:11
  23.9 12.3 %collective-permute-start.5 = (bf16[2,8,4992]{2,1,0:T(8,128)(2,1)S(1)}, bf16[2,8,4992]{2,1,0:T(8,128)(2,1)S(1)}, u32[]{:S(2)}, u32[]{:S(2)}) collective-permute-start(bf16[2,8,4992]{2,1,0:T(8,128)(2,1)S(1)} %get-tuple-element.40), channel_id=1, source_target_pairs={{0,12},{1,13},{2,14},{3,15},{4,8},{5,9},{6,10},{7,11},{8,4},{9,5},... | collective-permute-start | bytes 479240 | tf_op jit(solution)/shard_map/ppermute | solution.py:11
  24.2 12.0 %collective-permute-start.6 = (bf16[2,8,4992]{2,1,0:T(8,128)(2,1)S(1)}, bf16[2,8,4992]{2,1,0:T(8,128)(2,1)S(1)}, u32[]{:S(2)}, u32[]{:S(2)}) collective-permute-start(bf16[2,8,4992]{2,1,0:T(8,128)(2,1)S(1)} %get-tuple-element.39), channel_id=1, source_target_pairs={{0,8},{1,9},{2,10},{3,11},{4,12},{5,13},{6,14},{7,15},{8,0},{9,1},... | collective-permute-start | bytes 479240 | tf_op jit(solution)/shard_map/ppermute | solution.py:11
  26.8 9.7 %collective-permute-start.7 = (bf16[2,8,4992]{2,1,0:T(8,128)(2,1)S(1)}, bf16[2,8,4992]{2,1,0:T(8,128)(2,1)S(1)}, u32[]{:S(2)}, u32[]{:S(2)}) collective-permute-start(bf16[2,8,4992]{2,1,0:T(8,128)(2,1)S(1)} %get-tuple-element.38), channel_id=1, source_target_pairs={{0,4},{1,5},{2,6},{3,7},{4,0},{5,1},{6,2},{7,3},{8,12},{9,13},{10,... | collective-permute-start | bytes 479240 | tf_op jit(solution)/shard_map/ppermute | solution.py:11
  28.3 13.4 %collective-permute-start.12 = (bf16[2,8,4992]{2,1,0:T(8,128)(2,1)S(1)}, bf16[2,8,4992]{2,1,0:T(8,128)(2,1)S(1)}, u32[]{:S(2)}, u32[]{:S(2)}) collective-permute-start(bf16[2,8,4992]{2,1,0:T(8,128)(2,1)S(1)} %get-tuple-element.41), channel_id=1, source_target_pairs={{0,12},{1,13},{2,14},{3,15},{4,8},{5,9},{6,10},{7,11},{8,4},{9,5},... | collective-permute-start | bytes 479240 | tf_op jit(solution)/shard_map/ppermute | solution.py:11
  28.6 13.1 %collective-permute-start.13 = (bf16[2,8,4992]{2,1,0:T(8,128)(2,1)S(1)}, bf16[2,8,4992]{2,1,0:T(8,128)(2,1)S(1)}, u32[]{:S(2)}, u32[]{:S(2)}) collective-permute-start(bf16[2,8,4992]{2,1,0:T(8,128)(2,1)S(1)} %get-tuple-element.43), channel_id=1, source_target_pairs={{0,8},{1,9},{2,10},{3,11},{4,12},{5,13},{6,14},{7,15},{8,0},{9,1},... | collective-permute-start | bytes 479240 | tf_op jit(solution)/shard_map/ppermute | solution.py:11
  36.2 6.1 %collective-permute-start.14 = (bf16[2,8,4992]{2,1,0:T(8,128)(2,1)S(1)}, bf16[2,8,4992]{2,1,0:T(8,128)(2,1)S(1)}, u32[]{:S(2)}, u32[]{:S(2)}) collective-permute-start(bf16[2,8,4992]{2,1,0:T(8,128)(2,1)S(1)} %get-tuple-element.42), channel_id=1, source_target_pairs={{0,4},{1,5},{2,6},{3,7},{4,0},{5,1},{6,2},{7,3},{8,12},{9,13},{10,... | collective-permute-start | bytes 479240 | tf_op jit(solution)/shard_map/ppermute | solution.py:11
  36.6 11.0 %collective-permute-start.11 = (bf16[2,8,4992]{2,1,0:T(8,128)(2,1)S(1)}, bf16[2,8,4992]{2,1,0:T(8,128)(2,1)S(1)}, u32[]{:S(2)}, u32[]{:S(2)}) collective-permute-start(bf16[2,8,4992]{2,1,0:T(8,128)(2,1)S(1)} %fusion.47), channel_id=1, source_target_pairs={{0,2},{1,3},{2,0},{3,1},{4,6},{5,7},{6,4},{7,5},{8,10},{9,11},{10,... | collective-permute-start | bytes 479240 | tf_op jit(solution)/shard_map/ppermute | solution.py:11
  42.4 13.2 %collective-permute-start.18 = (bf16[2,8,4992]{2,1,0:T(8,128)(2,1)S(1)}, bf16[2,8,4992]{2,1,0:T(8,128)(2,1)S(1)}, u32[]{:S(2)}, u32[]{:S(2)}) collective-permute-start(bf16[2,8,4992]{2,1,0:T(8,128)(2,1)S(1)} %fusion.48), channel_id=1, source_target_pairs={{0,2},{1,3},{2,0},{3,1},{4,6},{5,7},{6,4},{7,5},{8,10},{9,11},{10,... | collective-permute-start | bytes 479240 | tf_op jit(solution)/shard_map/ppermute | solution.py:11
  47.8 12.6 %collective-permute-start.15 = (bf16[2,8,4992]{2,1,0:T(8,128)(2,1)S(1)}, bf16[2,8,4992]{2,1,0:T(8,128)(2,1)S(1)}, u32[]{:S(2)}, u32[]{:S(2)}) collective-permute-start(bf16[2,8,4992]{2,1,0:T(8,128)(2,1)S(1)} %get-tuple-element.53), channel_id=1, source_target_pairs={{0,4},{1,5},{2,6},{3,7},{4,0},{5,1},{6,2},{7,3},{8,12},{9,13},{10,... | collective-permute-start | bytes 479240 | tf_op jit(solution)/shard_map/ppermute | solution.py:11
  51.7 8.7 %collective-permute-start.16 = (bf16[2,8,4992]{2,1,0:T(8,128)(2,1)S(1)}, bf16[2,8,4992]{2,1,0:T(8,128)(2,1)S(1)}, u32[]{:S(2)}, u32[]{:S(2)}) collective-permute-start(bf16[2,8,4992]{2,1,0:T(8,128)(2,1)S(1)} %get-tuple-element.53), channel_id=1, source_target_pairs={{0,8},{1,9},{2,10},{3,11},{4,12},{5,13},{6,14},{7,15},{8,0},{9,1},... | collective-permute-start | bytes 479240 | tf_op jit(solution)/shard_map/ppermute | solution.py:11
  51.7 11.5 %collective-permute-start.17 = (bf16[2,8,4992]{2,1,0:T(8,128)(2,1)S(1)}, bf16[2,8,4992]{2,1,0:T(8,128)(2,1)S(1)}, u32[]{:S(2)}, u32[]{:S(2)}) collective-permute-start(bf16[2,8,4992]{2,1,0:T(8,128)(2,1)S(1)} %get-tuple-element.53), channel_id=1, source_target_pairs={{0,12},{1,13},{2,14},{3,15},{4,8},{5,9},{6,10},{7,11},{8,4},{9,5},... | collective-permute-start | bytes 479240 | tf_op jit(solution)/shard_map/ppermute | solution.py:11
  55.8 11.0 %collective-permute-start.21 = (bf16[2,8,4992]{2,1,0:T(8,128)(2,1)S(1)}, bf16[2,8,4992]{2,1,0:T(8,128)(2,1)S(1)}, u32[]{:S(2)}, u32[]{:S(2)}) collective-permute-start(bf16[2,8,4992]{2,1,0:T(8,128)(2,1)S(1)} %get-tuple-element.54), channel_id=1, source_target_pairs={{0,12},{1,13},{2,14},{3,15},{4,8},{5,9},{6,10},{7,11},{8,4},{9,5},... | collective-permute-start | bytes 479240 | tf_op jit(solution)/shard_map/ppermute | solution.py:11
  57.1 9.7 %collective-permute-start.22 = (bf16[2,8,4992]{2,1,0:T(8,128)(2,1)S(1)}, bf16[2,8,4992]{2,1,0:T(8,128)(2,1)S(1)}, u32[]{:S(2)}, u32[]{:S(2)}) collective-permute-start(bf16[2,8,4992]{2,1,0:T(8,128)(2,1)S(1)} %get-tuple-element.54), channel_id=1, source_target_pairs={{0,8},{1,9},{2,10},{3,11},{4,12},{5,13},{6,14},{7,15},{8,0},{9,1},... | collective-permute-start | bytes 479240 | tf_op jit(solution)/shard_map/ppermute | solution.py:11
  60.4 6.4 %collective-permute-start.23 = (bf16[2,8,4992]{2,1,0:T(8,128)(2,1)S(1)}, bf16[2,8,4992]{2,1,0:T(8,128)(2,1)S(1)}, u32[]{:S(2)}, u32[]{:S(2)}) collective-permute-start(bf16[2,8,4992]{2,1,0:T(8,128)(2,1)S(1)} %get-tuple-element.54), channel_id=1, source_target_pairs={{0,4},{1,5},{2,6},{3,7},{4,0},{5,1},{6,2},{7,3},{8,12},{9,13},{10,... | collective-permute-start | bytes 479240 | tf_op jit(solution)/shard_map/ppermute | solution.py:11
  63.3 3.8 %collective-permute-start.19 = (bf16[2,32,4992]{2,1,0:T(8,128)(2,1)S(1)}, bf16[2,32,4992]{2,1,0:T(8,128)(2,1)S(1)}, u32[]{:S(2)}, u32[]{:S(2)}) collective-permute-start(bf16[2,32,4992]{2,1,0:T(8,128)(2,1)S(1)} %pad_maximum_fusion.3), channel_id=1, source_target_pairs={{0,1},{1,0},{2,3},{3,2},{4,5},{5,4},{6,7},{7,6},{8,9},{9,8},{10,11... | collective-permute-start | bytes 1916936 | tf_op jit(solution)/shard_map/ppermute | solution.py:11
  66.9 2.2 %collective-permute-start.24 = (bf16[2,32,4992]{2,1,0:T(8,128)(2,1)S(1)}, bf16[2,32,4992]{2,1,0:T(8,128)(2,1)S(1)}, u32[]{:S(2)}, u32[]{:S(2)}) collective-permute-start(bf16[2,32,4992]{2,1,0:T(8,128)(2,1)S(1)} %pad_maximum_fusion.4), channel_id=1, source_target_pairs={{0,1},{1,0},{2,3},{3,2},{4,5},{5,4},{6,7},{7,6},{8,9},{9,8},{10,11... | collective-permute-start | bytes 1916936 | tf_op jit(solution)/shard_map/ppermute | solution.py:11
  70.0 10.1 %collective-permute-start.20 = (f32[64,512]{1,0:T(8,128)S(1)}, f32[64,512]{1,0:T(8,128)S(1)}, u32[]{:S(2)}, u32[]{:S(2)}) collective-permute-start(f32[64,512]{1,0:T(8,128)S(1)} %slice.267), channel_id=1, source_target_pairs={{0,32},{16,48},{32,0},{48,16},{64,96},{80,112},{96,64},{112,80},{1... | collective-permute-start | bytes 393224 | tf_op jit(solution)/shard_map/ppermute | solution.py:11
  73.5 6.6 %collective-permute-start.25 = (f32[64,512]{1,0:T(8,128)S(1)}, f32[64,512]{1,0:T(8,128)S(1)}, u32[]{:S(2)}, u32[]{:S(2)}) collective-permute-start(f32[64,512]{1,0:T(8,128)S(1)} %get-tuple-element.50), channel_id=1, source_target_pairs={{0,48},{16,32},{32,16},{48,0},{64,112},{80,96},{96,80},{112,64},{1... | collective-permute-start | bytes 393224 | tf_op jit(solution)/shard_map/ppermute | solution.py:11
  74.7 5.4 %collective-permute-start.26 = (f32[64,512]{1,0:T(8,128)S(1)}, f32[64,512]{1,0:T(8,128)S(1)}, u32[]{:S(2)}, u32[]{:S(2)}) collective-permute-start(f32[64,512]{1,0:T(8,128)S(1)} %get-tuple-element.51), channel_id=1, source_target_pairs={{0,16},{16,0},{32,48},{48,32},{64,80},{80,64},{96,112},{112,96},{1... | collective-permute-start | bytes 393224 | tf_op jit(solution)/shard_map/ppermute | solution.py:11
  80.3 6.4 %collective-permute-start.27 = (f32[16,512]{1,0:T(8,128)S(1)}, f32[16,512]{1,0:T(8,128)S(1)}, u32[]{:S(2)}, u32[]{:S(2)}) collective-permute-start(f32[16,512]{1,0:T(8,128)S(1)} %get-tuple-element.56), channel_id=1, source_target_pairs={{0,192},{16,208},{32,224},{48,240},{64,128},{80,144},{96,160},{112... | collective-permute-start | bytes 98312 | tf_op jit(solution)/shard_map/ppermute | solution.py:11
  81.8 5.1 %collective-permute-start.28 = (f32[16,512]{1,0:T(8,128)S(1)}, f32[16,512]{1,0:T(8,128)S(1)}, u32[]{:S(2)}, u32[]{:S(2)}) collective-permute-start(f32[16,512]{1,0:T(8,128)S(1)} %get-tuple-element.58), channel_id=1, source_target_pairs={{0,128},{16,144},{32,160},{48,176},{64,192},{80,208},{96,224},{112... | collective-permute-start | bytes 98312 | tf_op jit(solution)/shard_map/ppermute | solution.py:11
  81.8 5.2 %collective-permute-start.29 = (f32[16,512]{1,0:T(8,128)S(1)}, f32[16,512]{1,0:T(8,128)S(1)}, u32[]{:S(2)}, u32[]{:S(2)}) collective-permute-start(f32[16,512]{1,0:T(8,128)S(1)} %get-tuple-element.57), channel_id=1, source_target_pairs={{0,64},{16,80},{32,96},{48,112},{64,0},{80,16},{96,32},{112,48},{1... | collective-permute-start | bytes 98312 | tf_op jit(solution)/shard_map/ppermute | solution.py:11
  (1 other events, 4.5 us)
where the time goes:
time: 89 us; the launch traced here: 87.6 us
  starting transfers between devices  46.8 us (53%)
  waiting for transfers between devices  23 us (26%)
  matrix products  12.7 us (14%)
  other arithmetic  3.42 us (4%)
  between operations  1.15 us (1%)
    ppermute x30, starting transfers between devices, swapped(): return lambda a: lax.ppermute(a, axis, [(i, i ^ mask) for i in range(16)])  46.8 us
    ppermute x30, waiting for transfers between devices, swapped(): return lambda a: lax.ppermute(a, axis, [(i, i ^ mask) for i in range(16)])  23 us
    dot_general x16, matrix products, dot(): lax.dot_general(left, right, (dims, ((), ())), preferred_element_type=F32)  12.7 us
  transfers between devices with their start and end apart: 30, of which 16 were waited for; matrix products, arithmetic and copies ran while one was open for 16% of the time, Pallas kernels for 0%

commit v1 on v0

--- a/solution.py
+++ b/solution.py
@@ -64,7 +64,7 @@
     place = (col % 2) * 4 + col // 4
 
     both = side_by_side(tokens, out_grad)
-    own = jnp.concatenate([both] + [on_z_lo(k)(both) for k in (3, 2, 1)], axis=0)
+    own = jnp.concatenate([both] + [on_z_lo(k)(both) for k in (1, 2, 3)], axis=0)
     own = xor_blocks(own, place)
     near, far = on_x(2)(own), [on_x(1)(own), on_x(3)(own)]
 
@@ -82,8 +82,8 @@
     def reduced_on_core(part):
         return part[:, :32] + on_core(part[:, 32:])
 
-    def sent_on_y(pair):
-        return [pair[:, 8 * q : 8 * q + 8].astype(BF16) for q in (3, 2, 1)]
+    def sent_on_y(pair, order):
+        return [pair[:, 8 * q : 8 * q + 8].astype(BF16) for q in order]
 
     def reduced_on_y(pair, others):
         total = pair[:, :8]
@@ -104,12 +104,18 @@
         )
 
     part = partial_sums(own)
-    near = after(near, part)
-    part = jnp.concatenate((part, partial_sums(near)), axis=0)
-    far = jnp.concatenate(after(far, part), axis=0)
-    pairs = [reduced_on_core(part), reduced_on_core(partial_sums(far))]
-    sent = [sent_on_y(pair) for pair in pairs]
-    others = [[on_y(q)(block) for q, block in zip((3, 2, 1), blocks)] for blocks in sent]
+    pair = reduced_on_core(part)
+    rest = jnp.concatenate(after(far + [near], part), axis=0)
+    part = partial_sums(rest)
+    pairs = [
+        jnp.concatenate((pair, reduced_on_core(part[2:])), axis=0),
+        reduced_on_core(part[:2]),
+    ]
+    orders = ((1, 2, 3), (3, 1, 2))
+    sent = [sent_on_y(pair, order) for pair, order in zip(pairs, orders)]
+    others = [
+        [on_y(q)(block) for q, block in zip(order, blocks)] for order, blocks in zip(orders, sent)
+    ]
     totals = [
         reduced_on_y(pairs[0], after(others[0], sent[1])),
         reduced_on_y(pairs[1], others[1]),
@@ -119,8 +125,8 @@
     first = local(totals[0], after(others[0], sent[1]))
     second = local(totals[1], others[1])
     others = [
-        after([on_y(q)(first) for q in (1, 2, 3)], second),
-        after([on_y(q)(second) for q in (3, 2, 1)], first)[::-1],
+        after([on_y(q)(first) for q in (3, 2, 1)], second)[::-1],
+        after([on_y(q)(second) for q in (1, 2, 3)], first),
     ]
     halves = [jnp.concatenate([a] + b, axis=1) for a, b in zip((first, second), others)]
     others = [on_core(half) for half in halves]
@@ -133,11 +139,11 @@
     back_total = back_total + on_x(3)(back[64:]) + on_x(1)(back[:64])
     back_total = xor_blocks(back_total, place)
     total = back_total[:16]
-    for i, k in enumerate((3, 2, 1)):
-        total = total + on_z_lo(k)(back_total[16 * i + 16 : 16 * i + 32])
+    for k in (3, 1, 2):
+        total = total + on_z_lo(k)(back_total[16 * k : 16 * k + 16])
     input_grad = total.astype(BF16)
 
-    panel = jnp.concatenate((own, near, far), axis=0)
+    panel = jnp.concatenate((own, near, rest[:128]), axis=0)
     cots = after(jnp.concatenate(fulls, axis=0), back)
     factor = F32(panel.shape[0]) ** (-0.5)
     token, cot = panel[:, :depth], panel[:, depth:]

time: 89 us -> 88.7 us (level)
  waiting for transfers between devices: 23 us -> 26.8 us
  starting transfers between devices: 46.8 us -> 44.1 us
  matrix products: 12.7 us -> 11.5 us
    ppermute x30 -> x31, waiting for transfers between devices: 23 us -> 26.8 us  [swapped(): return lambda a: lax.ppermute(a, axis, [(i, i ^ mask) for i in range(16)])]
    ppermute x30 -> x31, starting transfers between devices: 46.8 us -> 44.1 us  [swapped(): return lambda a: lax.ppermute(a, axis, [(i, i ^ mask) for i in range(16)])]
    dot_general x16 -> x13, matrix products: 12.7 us -> 11.5 us  [dot(): lax.dot_general(left, right, (dims, ((), ())), preferred_element_type=F32)]
  transfers between devices with their start and end apart: 30 -> 31, of which waited for: 16 -> 14; matrix products, arithmetic and copies ran while one was open for 16% -> 16% of each run, Pallas kernels for 0% -> 0%
where the time goes in v1:
time: 88.7 us; the launch traced here: 87.6 us
  starting transfers between devices  44.1 us (50%)
  waiting for transfers between devices  26.8 us (30%)
  matrix products  11.5 us (13%)
  other arithmetic  3.37 us (4%)
  between operations  1.16 us (1%)
    ppermute x31, starting transfers between devices, swapped(): return lambda a: lax.ppermute(a, axis, [(i, i ^ mask) for i in range(16)])  44.1 us
    ppermute x31, waiting for transfers between devices, swapped(): return lambda a: lax.ppermute(a, axis, [(i, i ^ mask) for i in range(16)])  26.8 us
    dot_general x13, matrix products, dot(): lax.dot_general(left, right, (dims, ((), ())), preferred_element_type=F32)  11.5 us
  transfers between devices with their start and end apart: 31, of which 14 were waited for; matrix products, arithmetic and copies ran while one was open for 16% of the time, Pallas kernels for 0%

profile of v1, /device:TPU:24, one launch (start us, length us, event | category | flops | bytes accessed | tf_op | source)
XLA Modules:
  0.0 87.6 jit_solution(3500242463131399524)
XLA Ops:
  0.6 0.9 pad_add_fusion
  1.5 4.6 %collective-permute-start.2 = (bf16[16,1024]{1,0:T(8,128)(2,1)S(1)}, bf16[16,1024]{1,0:T(8,128)(2,1)S(1)}, u32[]{:S(2)}, u32[]{:S(2)}) collective-permute-start(bf16[16,1024]{1,0:T(8,128)(2,1)S(1)} %pad_add_fusion), channel_id=1, source_target_pairs={{0,192},{16,208},{32,224},{48,240},{64,128},{80,144},{96,160},{112... | collective-permute-start | bytes 98312 | tf_op jit(solution)/shard_map/ppermute | solution.py:11
  6.7 1.5 %collective-permute-done.2 = bf16[16,1024]{1,0:T(8,128)(2,1)S(1)} collective-permute-done((bf16[16,1024]{1,0:T(8,128)(2,1)S(1)}, bf16[16,1024]{1,0:T(8,128)(2,1)S(1)}, u32[]{:S(2)}, u32[]{:S(2)}) %collective-permute-start.2) | collective-permute-done | bytes 32800 | tf_op jit(solution)/shard_map/ppermute | solution.py:11
  8.2 2.7 %collective-permute-done.1 = bf16[16,1024]{1,0:T(8,128)(2,1)S(1)} collective-permute-done((bf16[16,1024]{1,0:T(8,128)(2,1)S(1)}, bf16[16,1024]{1,0:T(8,128)(2,1)S(1)}, u32[]{:S(2)}, u32[]{:S(2)}) %collective-permute-start.1) | collective-permute-done | bytes 32800 | tf_op jit(solution)/shard_map/ppermute | solution.py:11
  11.3 3.1 %collective-permute-start.6 = (bf16[64,1024]{1,0:T(8,128)(2,1)S(1)}, bf16[64,1024]{1,0:T(8,128)(2,1)S(1)}, u32[]{:S(2)}, u32[]{:S(2)}) collective-permute-start(bf16[64,1024]{1,0:T(8,128)(2,1)S(1)} %fusion.28), channel_id=1, source_target_pairs={{0,32},{16,48},{32,0},{48,16},{64,96},{80,112},{96,64},{112,80},{1... | collective-permute-start | bytes 393224 | tf_op jit(solution)/shard_map/ppermute | solution.py:11
  14.4 1.1 %collective-permute-start.5 = (bf16[64,1024]{1,0:T(8,128)(2,1)S(1)}, bf16[64,1024]{1,0:T(8,128)(2,1)S(1)}, u32[]{:S(2)}, u32[]{:S(2)}) collective-permute-start(bf16[64,1024]{1,0:T(8,128)(2,1)S(1)} %fusion.28), channel_id=1, source_target_pairs={{0,48},{16,32},{32,16},{48,0},{64,112},{80,96},{96,80},{112,64},{1... | collective-permute-start | bytes 393224 | tf_op jit(solution)/shard_map/ppermute | solution.py:11
  17.9 2.7 %collective-permute-done.5 = bf16[64,1024]{1,0:T(8,128)(2,1)S(1)} collective-permute-done((bf16[64,1024]{1,0:T(8,128)(2,1)S(1)}, bf16[64,1024]{1,0:T(8,128)(2,1)S(1)}, u32[]{:S(2)}, u32[]{:S(2)}) %collective-permute-start.5) | collective-permute-done | bytes 131104 | tf_op jit(solution)/shard_map/ppermute | solution.py:11
  21.2 0.7 fusion.19
  23.7 1.1 %collective-permute-done.7 = f32[1,32,4992]{2,1,0:T(8,128)S(1)} collective-permute-done((f32[1,32,4992]{2,1,0:T(8,128)S(1)}, f32[1,32,4992]{2,1,0:T(8,128)S(1)}, u32[]{:S(2)}, u32[]{:S(2)}) %collective-permute-start.7) | collective-permute-done | bytes 639008 | tf_op jit(solution)/shard_map/ppermute | solution.py:11
  25.3 2.6 %collective-permute-start.9 = (bf16[2,8,4992]{2,1,0:T(8,128)(2,1)S(1)}, bf16[2,8,4992]{2,1,0:T(8,128)(2,1)S(1)}, u32[]{:S(2)}, u32[]{:S(2)}) collective-permute-start(bf16[2,8,4992]{2,1,0:T(8,128)(2,1)S(1)} %get-tuple-element.39), channel_id=1, source_target_pairs={{0,8},{1,9},{2,10},{3,11},{4,12},{5,13},{6,14},{7,15},{8,0},{9,1},... | collective-permute-start | bytes 479240 | tf_op jit(solution)/shard_map/ppermute | solution.py:11
  27.9 1.3 %collective-permute-start.8 = (bf16[2,8,4992]{2,1,0:T(8,128)(2,1)S(1)}, bf16[2,8,4992]{2,1,0:T(8,128)(2,1)S(1)}, u32[]{:S(2)}, u32[]{:S(2)}) collective-permute-start(bf16[2,8,4992]{2,1,0:T(8,128)(2,1)S(1)} %get-tuple-element.40), channel_id=1, source_target_pairs={{0,4},{1,5},{2,6},{3,7},{4,0},{5,1},{6,2},{7,3},{8,12},{9,13},{10,... | collective-permute-start | bytes 479240 | tf_op jit(solution)/shard_map/ppermute | solution.py:11
  29.8 2.6 %collective-permute-start.15 = (bf16[2,8,4992]{2,1,0:T(8,128)(2,1)S(1)}, bf16[2,8,4992]{2,1,0:T(8,128)(2,1)S(1)}, u32[]{:S(2)}, u32[]{:S(2)}) collective-permute-start(bf16[2,8,4992]{2,1,0:T(8,128)(2,1)S(1)} %get-tuple-element.42), channel_id=1, source_target_pairs={{0,8},{1,9},{2,10},{3,11},{4,12},{5,13},{6,14},{7,15},{8,0},{9,1},... | collective-permute-start | bytes 479240 | tf_op jit(solution)/shard_map/ppermute | solution.py:11
  32.4 4.9 %collective-permute-done.10 = bf16[2,8,4992]{2,1,0:T(8,128)(2,1)S(1)} collective-permute-done((bf16[2,8,4992]{2,1,0:T(8,128)(2,1)S(1)}, bf16[2,8,4992]{2,1,0:T(8,128)(2,1)S(1)}, u32[]{:S(2)}, u32[]{:S(2)}) %collective-permute-start.10) | collective-permute-done | bytes 159776 | tf_op jit(solution)/shard_map/ppermute | solution.py:11
  37.7 4.8 %collective-permute-start.12 = (bf16[2,8,4992]{2,1,0:T(8,128)(2,1)S(1)}, bf16[2,8,4992]{2,1,0:T(8,128)(2,1)S(1)}, u32[]{:S(2)}, u32[]{:S(2)}) collective-permute-start(bf16[2,8,4992]{2,1,0:T(8,128)(2,1)S(1)} %get-tuple-element.34), channel_id=1, source_target_pairs={{0,2},{1,3},{2,0},{3,1},{4,6},{5,7},{6,4},{7,5},{8,10},{9,11},{10,... | collective-permute-start | bytes 479240 | tf_op jit(solution)/shard_map/ppermute | solution.py:11
  43.5 4.7 %collective-permute-start.19 = (bf16[2,8,4992]{2,1,0:T(8,128)(2,1)S(1)}, bf16[2,8,4992]{2,1,0:T(8,128)(2,1)S(1)}, u32[]{:S(2)}, u32[]{:S(2)}) collective-permute-start(bf16[2,8,4992]{2,1,0:T(8,128)(2,1)S(1)} %fusion.41), channel_id=1, source_target_pairs={{0,2},{1,3},{2,0},{3,1},{4,6},{5,7},{6,4},{7,5},{8,10},{9,11},{10,... | collective-permute-start | bytes 479240 | tf_op jit(solution)/shard_map/ppermute | solution.py:11
  48.3 1.8 %collective-permute-start.18 = (bf16[2,8,4992]{2,1,0:T(8,128)(2,1)S(1)}, bf16[2,8,4992]{2,1,0:T(8,128)(2,1)S(1)}, u32[]{:S(2)}, u32[]{:S(2)}) collective-permute-start(bf16[2,8,4992]{2,1,0:T(8,128)(2,1)S(1)} %get-tuple-element.53), channel_id=1, source_target_pairs={{0,4},{1,5},{2,6},{3,7},{4,0},{5,1},{6,2},{7,3},{8,12},{9,13},{10,... | collective-permute-start | bytes 479240 | tf_op jit(solution)/shard_map/ppermute | solution.py:11
  50.2 2.9 %collective-permute-start.16 = (bf16[2,8,4992]{2,1,0:T(8,128)(2,1)S(1)}, bf16[2,8,4992]{2,1,0:T(8,128)(2,1)S(1)}, u32[]{:S(2)}, u32[]{:S(2)}) collective-permute-start(bf16[2,8,4992]{2,1,0:T(8,128)(2,1)S(1)} %get-tuple-element.53), channel_id=1, source_target_pairs={{0,12},{1,13},{2,14},{3,15},{4,8},{5,9},{6,10},{7,11},{8,4},{9,5},... | collective-permute-start | bytes 479240 | tf_op jit(solution)/shard_map/ppermute | solution.py:11
  53.1 4.6 %collective-permute-done.19 = bf16[2,8,4992]{2,1,0:T(8,128)(2,1)S(1)} collective-permute-done((bf16[2,8,4992]{2,1,0:T(8,128)(2,1)S(1)}, bf16[2,8,4992]{2,1,0:T(8,128)(2,1)S(1)}, u32[]{:S(2)}, u32[]{:S(2)}) %collective-permute-start.19) | collective-permute-done | bytes 159776 | tf_op jit(solution)/shard_map/ppermute | solution.py:11
  58.3 1.7 %collective-permute-start.23 = (bf16[2,8,4992]{2,1,0:T(8,128)(2,1)S(1)}, bf16[2,8,4992]{2,1,0:T(8,128)(2,1)S(1)}, u32[]{:S(2)}, u32[]{:S(2)}) collective-permute-start(bf16[2,8,4992]{2,1,0:T(8,128)(2,1)S(1)} %get-tuple-element.54), channel_id=1, source_target_pairs={{0,8},{1,9},{2,10},{3,11},{4,12},{5,13},{6,14},{7,15},{8,0},{9,1},... | collective-permute-start | bytes 479240 | tf_op jit(solution)/shard_map/ppermute | solution.py:11
  60.0 2.1 %collective-permute-start.22 = (bf16[2,8,4992]{2,1,0:T(8,128)(2,1)S(1)}, bf16[2,8,4992]{2,1,0:T(8,128)(2,1)S(1)}, u32[]{:S(2)}, u32[]{:S(2)}) collective-permute-start(bf16[2,8,4992]{2,1,0:T(8,128)(2,1)S(1)} %get-tuple-element.54), channel_id=1, source_target_pairs={{0,4},{1,5},{2,6},{3,7},{4,0},{5,1},{6,2},{7,3},{8,12},{9,13},{10,... | collective-permute-start | bytes 479240 | tf_op jit(solution)/shard_map/ppermute | solution.py:11
  62.3 5.1 %collective-permute-done.24 = bf16[2,8,4992]{2,1,0:T(8,128)(2,1)S(1)} collective-permute-done((bf16[2,8,4992]{2,1,0:T(8,128)(2,1)S(1)}, bf16[2,8,4992]{2,1,0:T(8,128)(2,1)S(1)}, u32[]{:S(2)}, u32[]{:S(2)}) %collective-permute-start.24) | collective-permute-done | bytes 159776 | tf_op jit(solution)/shard_map/ppermute | solution.py:11
  69.0 0.7 convolution_add_fusion.1
  69.7 1.6 %collective-permute-start.21 = (f32[64,512]{1,0:T(8,128)S(1)}, f32[64,512]{1,0:T(8,128)S(1)}, u32[]{:S(2)}, u32[]{:S(2)}) collective-permute-start(f32[64,512]{1,0:T(8,128)S(1)} %slice.286), channel_id=1, source_target_pairs={{0,32},{16,48},{32,0},{48,16},{64,96},{80,112},{96,64},{112,80},{1... | collective-permute-start | bytes 393224 | tf_op jit(solution)/shard_map/ppermute | solution.py:11
  71.4 0.7 fusion.5
  73.0 1.1 %collective-permute-start.26 = (f32[64,512]{1,0:T(8,128)S(1)}, f32[64,512]{1,0:T(8,128)S(1)}, u32[]{:S(2)}, u32[]{:S(2)}) collective-permute-start(f32[64,512]{1,0:T(8,128)S(1)} %get-tuple-element.50), channel_id=1, source_target_pairs={{0,48},{16,32},{32,16},{48,0},{64,112},{80,96},{96,80},{112,64},{1... | collective-permute-start | bytes 393224 | tf_op jit(solution)/shard_map/ppermute | solution.py:11
  74.0 1.0 %collective-permute-start.27 = (f32[64,512]{1,0:T(8,128)S(1)}, f32[64,512]{1,0:T(8,128)S(1)}, u32[]{:S(2)}, u32[]{:S(2)}) collective-permute-start(f32[64,512]{1,0:T(8,128)S(1)} %get-tuple-element.51), channel_id=1, source_target_pairs={{0,16},{16,0},{32,48},{48,32},{64,80},{80,64},{96,112},{112,96},{1... | collective-permute-start | bytes 393224 | tf_op jit(solution)/shard_map/ppermute | solution.py:11
  75.1 1.8 %multiply_convert_fusion = bf16[1664,512]{1,0:T(8,128)(2,1)} fusion(bf16[256,4992]{1,0:T(8,128)(2,1)S(1)} %pad_maximum_fusion.2, bf16[256,1024]{1,0:T(8,128)(2,1)S(1)} %pad_maximum_fusion.6), kind=kOutput, calls=%fused_computation | convolution fusion | flops 437911552 | bytes 2818048 | tf_op jit(solution)/shard_map/dot_general | solution.py:47
  76.9 1.9 %multiply_convert_fusion.1 = bf16[512,1664]{1,0:T(8,128)(2,1)} fusion(bf16[256,4992]{1,0:T(8,128)(2,1)S(1)} %pad_maximum_fusion.2, bf16[256,1024]{1,0:T(8,128)(2,1)S(1)} %pad_maximum_fusion.6), kind=kOutput, calls=%fused_computation.1 | convolution fusion | flops 437911552 | bytes 2818048 | tf_op jit(solution)/shard_map/dot_general | solution.py:47
  78.8 1.3 %collective-permute-done.26 = f32[64,512]{1,0:T(8,128)S(1)} collective-permute-done((f32[64,512]{1,0:T(8,128)S(1)}, f32[64,512]{1,0:T(8,128)S(1)}, u32[]{:S(2)}, u32[]{:S(2)}) %collective-permute-start.26) | collective-permute-done | bytes 131104 | tf_op jit(solution)/shard_map/ppermute | solution.py:11
  80.3 1.8 %collective-permute-start.28 = (f32[16,512]{1,0:T(8,128)S(1)}, f32[16,512]{1,0:T(8,128)S(1)}, u32[]{:S(2)}, u32[]{:S(2)}) collective-permute-start(f32[16,512]{1,0:T(8,128)S(1)} %get-tuple-element.56), channel_id=1, source_target_pairs={{0,192},{16,208},{32,224},{48,240},{64,128},{80,144},{96,160},{112... | collective-permute-start | bytes 98312 | tf_op jit(solution)/shard_map/ppermute | solution.py:11
  82.0 2.7 %collective-permute-start.29 = (f32[16,512]{1,0:T(8,128)S(1)}, f32[16,512]{1,0:T(8,128)S(1)}, u32[]{:S(2)}, u32[]{:S(2)}) collective-permute-start(f32[16,512]{1,0:T(8,128)S(1)} %get-tuple-element.58), channel_id=1, source_target_pairs={{0,64},{16,80},{32,96},{48,112},{64,0},{80,16},{96,32},{112,48},{1... | collective-permute-start | bytes 98312 | tf_op jit(solution)/shard_map/ppermute | solution.py:11
  84.7 1.9 %multiply_convert_fusion.2 = bf16[512,1664]{1,0:T(8,128)(2,1)} fusion(bf16[256,4992]{1,0:T(8,128)(2,1)S(1)} %pad_maximum_fusion.2, bf16[256,1024]{1,0:T(8,128)(2,1)S(1)} %pad_maximum_fusion.6), kind=kOutput, calls=%fused_computation.2 | convolution fusion | flops 437911552 | bytes 2818048 | tf_op jit(solution)/shard_map/dot_general | solution.py:47
  (106 shorter events, 12.6 us)
Async XLA Ops:
  0.6 16.0 %copy-start = (bf16[512,1664]{1,0:T(8,128)(2,1)S(1)}, bf16[512,1664]{1,0:T(8,128)(2,1)}, u32[]{:S(2)}) copy-start(bf16[512,1664]{1,0:T(8,128)(2,1)} %param.6) | copy-start | bytes 5111812
  1.5 6.7 %collective-permute-start.2 = (bf16[16,1024]{1,0:T(8,128)(2,1)S(1)}, bf16[16,1024]{1,0:T(8,128)(2,1)S(1)}, u32[]{:S(2)}, u32[]{:S(2)}) collective-permute-start(bf16[16,1024]{1,0:T(8,128)(2,1)S(1)} %pad_add_fusion), channel_id=1, source_target_pairs={{0,192},{16,208},{32,224},{48,240},{64,128},{80,144},{96,160},{112... | collective-permute-start | bytes 98312 | tf_op jit(solution)/shard_map/ppermute | solution.py:11
  6.1 4.8 %collective-permute-start.1 = (bf16[16,1024]{1,0:T(8,128)(2,1)S(1)}, bf16[16,1024]{1,0:T(8,128)(2,1)S(1)}, u32[]{:S(2)}, u32[]{:S(2)}) collective-permute-start(bf16[16,1024]{1,0:T(8,128)(2,1)S(1)} %pad_add_fusion), channel_id=1, source_target_pairs={{0,128},{16,144},{32,160},{48,176},{64,192},{80,208},{96,224},{112... | collective-permute-start | bytes 98312 | tf_op jit(solution)/shard_map/ppermute | solution.py:11
  6.1 4.8 %collective-permute-start = (bf16[16,1024]{1,0:T(8,128)(2,1)S(1)}, bf16[16,1024]{1,0:T(8,128)(2,1)S(1)}, u32[]{:S(2)}, u32[]{:S(2)}) collective-permute-start(bf16[16,1024]{1,0:T(8,128)(2,1)S(1)} %pad_add_fusion), channel_id=1, source_target_pairs={{0,64},{16,80},{32,96},{48,112},{64,0},{80,16},{96,32},{112,48},{1... | collective-permute-start | bytes 98312 | tf_op jit(solution)/shard_map/ppermute | solution.py:11
  11.3 6.7 %collective-permute-start.6 = (bf16[64,1024]{1,0:T(8,128)(2,1)S(1)}, bf16[64,1024]{1,0:T(8,128)(2,1)S(1)}, u32[]{:S(2)}, u32[]{:S(2)}) collective-permute-start(bf16[64,1024]{1,0:T(8,128)(2,1)S(1)} %fusion.28), channel_id=1, source_target_pairs={{0,32},{16,48},{32,0},{48,16},{64,96},{80,112},{96,64},{112,80},{1... | collective-permute-start | bytes 393224 | tf_op jit(solution)/shard_map/ppermute | solution.py:11
  14.4 6.3 %collective-permute-start.5 = (bf16[64,1024]{1,0:T(8,128)(2,1)S(1)}, bf16[64,1024]{1,0:T(8,128)(2,1)S(1)}, u32[]{:S(2)}, u32[]{:S(2)}) collective-permute-start(bf16[64,1024]{1,0:T(8,128)(2,1)S(1)} %fusion.28), channel_id=1, source_target_pairs={{0,48},{16,32},{32,16},{48,0},{64,112},{80,96},{96,80},{112,64},{1... | collective-permute-start | bytes 393224 | tf_op jit(solution)/shard_map/ppermute | solution.py:11
  15.5 5.1 %collective-permute-start.4 = (bf16[64,1024]{1,0:T(8,128)(2,1)S(1)}, bf16[64,1024]{1,0:T(8,128)(2,1)S(1)}, u32[]{:S(2)}, u32[]{:S(2)}) collective-permute-start(bf16[64,1024]{1,0:T(8,128)(2,1)S(1)} %fusion.28), channel_id=1, source_target_pairs={{0,16},{16,0},{32,48},{48,32},{64,80},{80,64},{96,112},{112,96},{1... | collective-permute-start | bytes 393224 | tf_op jit(solution)/shard_map/ppermute | solution.py:11
  17.2 6.5 %collective-permute-start.3 = (f32[1,32,4992]{2,1,0:T(8,128)S(1)}, f32[1,32,4992]{2,1,0:T(8,128)S(1)}, u32[]{:S(2)}, u32[]{:S(2)}) collective-permute-start(f32[1,32,4992]{2,1,0:T(8,128)S(1)} %slice.261), channel_id=1, source_target_pairs={{0,1},{1,0},{2,3},{3,2},{4,5},{5,4},{6,7},{7,6},{8,9},{9,8},{10,11... | collective-permute-start | bytes 1916936 | tf_op jit(solution)/shard_map/ppermute | solution.py:11
  22.6 2.2 %collective-permute-start.7 = (f32[1,32,4992]{2,1,0:T(8,128)S(1)}, f32[1,32,4992]{2,1,0:T(8,128)S(1)}, u32[]{:S(2)}, u32[]{:S(2)}) collective-permute-start(f32[1,32,4992]{2,1,0:T(8,128)S(1)} %slice.265), channel_id=1, source_target_pairs={{0,1},{1,0},{2,3},{3,2},{4,5},{5,4},{6,7},{7,6},{8,9},{9,8},{10,11... | collective-permute-start | bytes 1916936 | tf_op jit(solution)/shard_map/ppermute | solution.py:11
  23.0 6.2 %collective-permute-start.11 = (f32[2,32,4992]{2,1,0:T(8,128)S(1)}, f32[2,32,4992]{2,1,0:T(8,128)S(1)}, u32[]{:S(2)}, u32[]{:S(2)}) collective-permute-start(f32[2,32,4992]{2,1,0:T(8,128)S(1)} %slice.272), channel_id=1, source_target_pairs={{0,1},{1,0},{2,3},{3,2},{4,5},{5,4},{6,7},{7,6},{8,9},{9,8},{10,11... | collective-permute-start | bytes 3833864 | tf_op jit(solution)/shard_map/ppermute | solution.py:11
  25.0 12.3 %collective-permute-start.10 = (bf16[2,8,4992]{2,1,0:T(8,128)(2,1)S(1)}, bf16[2,8,4992]{2,1,0:T(8,128)(2,1)S(1)}, u32[]{:S(2)}, u32[]{:S(2)}) collective-permute-start(bf16[2,8,4992]{2,1,0:T(8,128)(2,1)S(1)} %get-tuple-element.38), channel_id=1, source_target_pairs={{0,12},{1,13},{2,14},{3,15},{4,8},{5,9},{6,10},{7,11},{8,4},{9,5},... | collective-permute-start | bytes 479240 | tf_op jit(solution)/shard_map/ppermute | solution.py:11
  25.3 12.0 %collective-permute-start.9 = (bf16[2,8,4992]{2,1,0:T(8,128)(2,1)S(1)}, bf16[2,8,4992]{2,1,0:T(8,128)(2,1)S(1)}, u32[]{:S(2)}, u32[]{:S(2)}) collective-permute-start(bf16[2,8,4992]{2,1,0:T(8,128)(2,1)S(1)} %get-tuple-element.39), channel_id=1, source_target_pairs={{0,8},{1,9},{2,10},{3,11},{4,12},{5,13},{6,14},{7,15},{8,0},{9,1},... | collective-permute-start | bytes 479240 | tf_op jit(solution)/shard_map/ppermute | solution.py:11
  27.9 9.7 %collective-permute-start.8 = (bf16[2,8,4992]{2,1,0:T(8,128)(2,1)S(1)}, bf16[2,8,4992]{2,1,0:T(8,128)(2,1)S(1)}, u32[]{:S(2)}, u32[]{:S(2)}) collective-permute-start(bf16[2,8,4992]{2,1,0:T(8,128)(2,1)S(1)} %get-tuple-element.40), channel_id=1, source_target_pairs={{0,4},{1,5},{2,6},{3,7},{4,0},{5,1},{6,2},{7,3},{8,12},{9,13},{10,... | collective-permute-start | bytes 479240 | tf_op jit(solution)/shard_map/ppermute | solution.py:11
  29.5 13.3 %collective-permute-start.13 = (bf16[2,8,4992]{2,1,0:T(8,128)(2,1)S(1)}, bf16[2,8,4992]{2,1,0:T(8,128)(2,1)S(1)}, u32[]{:S(2)}, u32[]{:S(2)}) collective-permute-start(bf16[2,8,4992]{2,1,0:T(8,128)(2,1)S(1)} %get-tuple-element.41), channel_id=1, source_target_pairs={{0,12},{1,13},{2,14},{3,15},{4,8},{5,9},{6,10},{7,11},{8,4},{9,5},... | collective-permute-start | bytes 479240 | tf_op jit(solution)/shard_map/ppermute | solution.py:11
  29.8 13.0 %collective-permute-start.15 = (bf16[2,8,4992]{2,1,0:T(8,128)(2,1)S(1)}, bf16[2,8,4992]{2,1,0:T(8,128)(2,1)S(1)}, u32[]{:S(2)}, u32[]{:S(2)}) collective-permute-start(bf16[2,8,4992]{2,1,0:T(8,128)(2,1)S(1)} %get-tuple-element.42), channel_id=1, source_target_pairs={{0,8},{1,9},{2,10},{3,11},{4,12},{5,13},{6,14},{7,15},{8,0},{9,1},... | collective-permute-start | bytes 479240 | tf_op jit(solution)/shard_map/ppermute | solution.py:11
  37.3 6.1 %collective-permute-start.14 = (bf16[2,8,4992]{2,1,0:T(8,128)(2,1)S(1)}, bf16[2,8,4992]{2,1,0:T(8,128)(2,1)S(1)}, u32[]{:S(2)}, u32[]{:S(2)}) collective-permute-start(bf16[2,8,4992]{2,1,0:T(8,128)(2,1)S(1)} %get-tuple-element.43), channel_id=1, source_target_pairs={{0,4},{1,5},{2,6},{3,7},{4,0},{5,1},{6,2},{7,3},{8,12},{9,13},{10,... | collective-permute-start | bytes 479240 | tf_op jit(solution)/shard_map/ppermute | solution.py:11
  37.7 10.5 %collective-permute-start.12 = (bf16[2,8,4992]{2,1,0:T(8,128)(2,1)S(1)}, bf16[2,8,4992]{2,1,0:T(8,128)(2,1)S(1)}, u32[]{:S(2)}, u32[]{:S(2)}) collective-permute-start(bf16[2,8,4992]{2,1,0:T(8,128)(2,1)S(1)} %get-tuple-element.34), channel_id=1, source_target_pairs={{0,2},{1,3},{2,0},{3,1},{4,6},{5,7},{6,4},{7,5},{8,10},{9,11},{10,... | collective-permute-start | bytes 479240 | tf_op jit(solution)/shard_map/ppermute | solution.py:11
  43.5 14.2 %collective-permute-start.19 = (bf16[2,8,4992]{2,1,0:T(8,128)(2,1)S(1)}, bf16[2,8,4992]{2,1,0:T(8,128)(2,1)S(1)}, u32[]{:S(2)}, u32[]{:S(2)}) collective-permute-start(bf16[2,8,4992]{2,1,0:T(8,128)(2,1)S(1)} %fusion.41), channel_id=1, source_target_pairs={{0,2},{1,3},{2,0},{3,1},{4,6},{5,7},{6,4},{7,5},{8,10},{9,11},{10,... | collective-permute-start | bytes 479240 | tf_op jit(solution)/shard_map/ppermute | solution.py:11
  48.3 11.7 %collective-permute-start.18 = (bf16[2,8,4992]{2,1,0:T(8,128)(2,1)S(1)}, bf16[2,8,4992]{2,1,0:T(8,128)(2,1)S(1)}, u32[]{:S(2)}, u32[]{:S(2)}) collective-permute-start(bf16[2,8,4992]{2,1,0:T(8,128)(2,1)S(1)} %get-tuple-element.53), channel_id=1, source_target_pairs={{0,4},{1,5},{2,6},{3,7},{4,0},{5,1},{6,2},{7,3},{8,12},{9,13},{10,... | collective-permute-start | bytes 479240 | tf_op jit(solution)/shard_map/ppermute | solution.py:11
  50.0 12.0 %collective-permute-start.17 = (bf16[2,8,4992]{2,1,0:T(8,128)(2,1)S(1)}, bf16[2,8,4992]{2,1,0:T(8,128)(2,1)S(1)}, u32[]{:S(2)}, u32[]{:S(2)}) collective-permute-start(bf16[2,8,4992]{2,1,0:T(8,128)(2,1)S(1)} %get-tuple-element.53), channel_id=1, source_target_pairs={{0,8},{1,9},{2,10},{3,11},{4,12},{5,13},{6,14},{7,15},{8,0},{9,1},... | collective-permute-start | bytes 479240 | tf_op jit(solution)/shard_map/ppermute | solution.py:11
  50.2 11.9 %collective-permute-start.16 = (bf16[2,8,4992]{2,1,0:T(8,128)(2,1)S(1)}, bf16[2,8,4992]{2,1,0:T(8,128)(2,1)S(1)}, u32[]{:S(2)}, u32[]{:S(2)}) collective-permute-start(bf16[2,8,4992]{2,1,0:T(8,128)(2,1)S(1)} %get-tuple-element.53), channel_id=1, source_target_pairs={{0,12},{1,13},{2,14},{3,15},{4,8},{5,9},{6,10},{7,11},{8,4},{9,5},... | collective-permute-start | bytes 479240 | tf_op jit(solution)/shard_map/ppermute | solution.py:11
  57.9 9.5 %collective-permute-start.24 = (bf16[2,8,4992]{2,1,0:T(8,128)(2,1)S(1)}, bf16[2,8,4992]{2,1,0:T(8,128)(2,1)S(1)}, u32[]{:S(2)}, u32[]{:S(2)}) collective-permute-start(bf16[2,8,4992]{2,1,0:T(8,128)(2,1)S(1)} %get-tuple-element.54), channel_id=1, source_target_pairs={{0,12},{1,13},{2,14},{3,15},{4,8},{5,9},{6,10},{7,11},{8,4},{9,5},... | collective-permute-start | bytes 479240 | tf_op jit(solution)/shard_map/ppermute | solution.py:11
  58.3 9.1 %collective-permute-start.23 = (bf16[2,8,4992]{2,1,0:T(8,128)(2,1)S(1)}, bf16[2,8,4992]{2,1,0:T(8,128)(2,1)S(1)}, u32[]{:S(2)}, u32[]{:S(2)}) collective-permute-start(bf16[2,8,4992]{2,1,0:T(8,128)(2,1)S(1)} %get-tuple-element.54), channel_id=1, source_target_pairs={{0,8},{1,9},{2,10},{3,11},{4,12},{5,13},{6,14},{7,15},{8,0},{9,1},... | collective-permute-start | bytes 479240 | tf_op jit(solution)/shard_map/ppermute | solution.py:11
  60.0 8.0 %collective-permute-start.22 = (bf16[2,8,4992]{2,1,0:T(8,128)(2,1)S(1)}, bf16[2,8,4992]{2,1,0:T(8,128)(2,1)S(1)}, u32[]{:S(2)}, u32[]{:S(2)}) collective-permute-start(bf16[2,8,4992]{2,1,0:T(8,128)(2,1)S(1)} %get-tuple-element.54), channel_id=1, source_target_pairs={{0,4},{1,5},{2,6},{3,7},{4,0},{5,1},{6,2},{7,3},{8,12},{9,13},{10,... | collective-permute-start | bytes 479240 | tf_op jit(solution)/shard_map/ppermute | solution.py:11
  62.2 6.1 %collective-permute-start.20 = (bf16[2,32,4992]{2,1,0:T(8,128)(2,1)S(1)}, bf16[2,32,4992]{2,1,0:T(8,128)(2,1)S(1)}, u32[]{:S(2)}, u32[]{:S(2)}) collective-permute-start(bf16[2,32,4992]{2,1,0:T(8,128)(2,1)S(1)} %pad_maximum_fusion.4), channel_id=1, source_target_pairs={{0,1},{1,0},{2,3},{3,2},{4,5},{5,4},{6,7},{7,6},{8,9},{9,8},{10,11... | collective-permute-start | bytes 1916936 | tf_op jit(solution)/shard_map/ppermute | solution.py:11
  68.1 3.2 %collective-permute-start.25 = (bf16[2,32,4992]{2,1,0:T(8,128)(2,1)S(1)}, bf16[2,32,4992]{2,1,0:T(8,128)(2,1)S(1)}, u32[]{:S(2)}, u32[]{:S(2)}) collective-permute-start(bf16[2,32,4992]{2,1,0:T(8,128)(2,1)S(1)} %pad_maximum_fusion.5), channel_id=1, source_target_pairs={{0,1},{1,0},{2,3},{3,2},{4,5},{5,4},{6,7},{7,6},{8,9},{9,8},{10,11... | collective-permute-start | bytes 1916936 | tf_op jit(solution)/shard_map/ppermute | solution.py:11
  69.7 9.0 %collective-permute-start.21 = (f32[64,512]{1,0:T(8,128)S(1)}, f32[64,512]{1,0:T(8,128)S(1)}, u32[]{:S(2)}, u32[]{:S(2)}) collective-permute-start(f32[64,512]{1,0:T(8,128)S(1)} %slice.286), channel_id=1, source_target_pairs={{0,32},{16,48},{32,0},{48,16},{64,96},{80,112},{96,64},{112,80},{1... | collective-permute-start | bytes 393224 | tf_op jit(solution)/shard_map/ppermute | solution.py:11
  73.0 7.0 %collective-permute-start.26 = (f32[64,512]{1,0:T(8,128)S(1)}, f32[64,512]{1,0:T(8,128)S(1)}, u32[]{:S(2)}, u32[]{:S(2)}) collective-permute-start(f32[64,512]{1,0:T(8,128)S(1)} %get-tuple-element.50), channel_id=1, source_target_pairs={{0,48},{16,32},{32,16},{48,0},{64,112},{80,96},{96,80},{112,64},{1... | collective-permute-start | bytes 393224 | tf_op jit(solution)/shard_map/ppermute | solution.py:11
  74.0 6.0 %collective-permute-start.27 = (f32[64,512]{1,0:T(8,128)S(1)}, f32[64,512]{1,0:T(8,128)S(1)}, u32[]{:S(2)}, u32[]{:S(2)}) collective-permute-start(f32[64,512]{1,0:T(8,128)S(1)} %get-tuple-element.51), channel_id=1, source_target_pairs={{0,16},{16,0},{32,48},{48,32},{64,80},{80,64},{96,112},{112,96},{1... | collective-permute-start | bytes 393224 | tf_op jit(solution)/shard_map/ppermute | solution.py:11
  80.3 6.4 %collective-permute-start.28 = (f32[16,512]{1,0:T(8,128)S(1)}, f32[16,512]{1,0:T(8,128)S(1)}, u32[]{:S(2)}, u32[]{:S(2)}) collective-permute-start(f32[16,512]{1,0:T(8,128)S(1)} %get-tuple-element.56), channel_id=1, source_target_pairs={{0,192},{16,208},{32,224},{48,240},{64,128},{80,144},{96,160},{112... | collective-permute-start | bytes 98312 | tf_op jit(solution)/shard_map/ppermute | solution.py:11
  82.0 4.9 %collective-permute-start.30 = (f32[16,512]{1,0:T(8,128)S(1)}, f32[16,512]{1,0:T(8,128)S(1)}, u32[]{:S(2)}, u32[]{:S(2)}) collective-permute-start(f32[16,512]{1,0:T(8,128)S(1)} %get-tuple-element.57), channel_id=1, source_target_pairs={{0,128},{16,144},{32,160},{48,176},{64,192},{80,208},{96,224},{112... | collective-permute-start | bytes 98312 | tf_op jit(solution)/shard_map/ppermute | solution.py:11
  82.0 4.9 %collective-permute-start.29 = (f32[16,512]{1,0:T(8,128)S(1)}, f32[16,512]{1,0:T(8,128)S(1)}, u32[]{:S(2)}, u32[]{:S(2)}) collective-permute-start(f32[16,512]{1,0:T(8,128)S(1)} %get-tuple-element.58), channel_id=1, source_target_pairs={{0,64},{16,80},{32,96},{48,112},{64,0},{80,16},{96,32},{112,48},{1... | collective-permute-start | bytes 98312 | tf_op jit(solution)/shard_map/ppermute | solution.py:11
  (2 other events, 9.3 us)

commit v2 on v1

--- a/solution.py
+++ b/solution.py
@@ -55,6 +55,10 @@
 
 def after(value, other):
     return lax.optimization_barrier((value, other))[0]
+
+
+def in_order(values, order):
+    return [values[order.index(k)] for k in (1, 2, 3)]
 
 
 def body(tokens, gate_weight, up_weight, down_weight, out_grad):
@@ -125,8 +129,8 @@
     first = local(totals[0], after(others[0], sent[1]))
     second = local(totals[1], others[1])
     others = [
-        after([on_y(q)(first) for q in (3, 2, 1)], second)[::-1],
-        after([on_y(q)(second) for q in (1, 2, 3)], first),
+        in_order(after([on_y(q)(first) for q in (2, 1, 3)], second), (2, 1, 3)),
+        in_order(after([on_y(q)(second) for q in (2, 1, 3)], first), (2, 1, 3)),
     ]
     halves = [jnp.concatenate([a] + b, axis=1) for a, b in zip((first, second), others)]
     others = [on_core(half) for half in halves]

time: 88.7 us -> 88.4 us (level); the launches traced: 87.6 us -> 88.2 us
  transfers between devices with their start and end apart: 31 -> 31, of which waited for: 14 -> 14; matrix products, arithmetic and copies ran while one was open for 16% -> 15% of each run, Pallas kernels for 0% -> 0%
where the time goes in v2:
time: 88.4 us; the launch traced here: 88.2 us
  starting transfers between devices  44.7 us (51%)
  waiting for transfers between devices  26.8 us (30%)
  matrix products  11.5 us (13%)
  other arithmetic  3.36 us (4%)
  between operations  1.16 us (1%)
    ppermute x31, starting transfers between devices, swapped(): return lambda a: lax.ppermute(a, axis, [(i, i ^ mask) for i in range(16)])  44.7 us
    ppermute x31, waiting for transfers between devices, swapped(): return lambda a: lax.ppermute(a, axis, [(i, i ^ mask) for i in range(16)])  26.8 us
    dot_general x13, matrix products, dot(): lax.dot_general(left, right, (dims, ((), ())), preferred_element_type=F32)  11.5 us
  transfers between devices with their start and end apart: 31, of which 14 were waited for; matrix products, arithmetic and copies ran while one was open for 15% of the time, Pallas kernels for 0%

profile of v2, /device:TPU:24, one launch (start us, length us, event | category | flops | bytes accessed | tf_op | source)
XLA Modules:
  0.0 88.2 jit_solution(10582761136458070446)
XLA Ops:
  0.6 0.9 pad_add_fusion
  1.5 4.6 %collective-permute-start.2 = (bf16[16,1024]{1,0:T(8,128)(2,1)S(1)}, bf16[16,1024]{1,0:T(8,128)(2,1)S(1)}, u32[]{:S(2)}, u32[]{:S(2)}) collective-permute-start(bf16[16,1024]{1,0:T(8,128)(2,1)S(1)} %pad_add_fusion), channel_id=1, source_target_pairs={{0,192},{16,208},{32,224},{48,240},{64,128},{80,144},{96,160},{112... | collective-permute-start | bytes 98312 | tf_op jit(solution)/shard_map/ppermute | solution.py:11
  6.7 1.5 %collective-permute-done.2 = bf16[16,1024]{1,0:T(8,128)(2,1)S(1)} collective-permute-done((bf16[16,1024]{1,0:T(8,128)(2,1)S(1)}, bf16[16,1024]{1,0:T(8,128)(2,1)S(1)}, u32[]{:S(2)}, u32[]{:S(2)}) %collective-permute-start.2) | collective-permute-done | bytes 32800 | tf_op jit(solution)/shard_map/ppermute | solution.py:11
  8.2 2.7 %collective-permute-done.1 = bf16[16,1024]{1,0:T(8,128)(2,1)S(1)} collective-permute-done((bf16[16,1024]{1,0:T(8,128)(2,1)S(1)}, bf16[16,1024]{1,0:T(8,128)(2,1)S(1)}, u32[]{:S(2)}, u32[]{:S(2)}) %collective-permute-start.1) | collective-permute-done | bytes 32800 | tf_op jit(solution)/shard_map/ppermute | solution.py:11
  11.3 3.1 %collective-permute-start.6 = (bf16[64,1024]{1,0:T(8,128)(2,1)S(1)}, bf16[64,1024]{1,0:T(8,128)(2,1)S(1)}, u32[]{:S(2)}, u32[]{:S(2)}) collective-permute-start(bf16[64,1024]{1,0:T(8,128)(2,1)S(1)} %fusion.28), channel_id=1, source_target_pairs={{0,32},{16,48},{32,0},{48,16},{64,96},{80,112},{96,64},{112,80},{1... | collective-permute-start | bytes 393224 | tf_op jit(solution)/shard_map/ppermute | solution.py:11
  14.4 1.1 %collective-permute-start.5 = (bf16[64,1024]{1,0:T(8,128)(2,1)S(1)}, bf16[64,1024]{1,0:T(8,128)(2,1)S(1)}, u32[]{:S(2)}, u32[]{:S(2)}) collective-permute-start(bf16[64,1024]{1,0:T(8,128)(2,1)S(1)} %fusion.28), channel_id=1, source_target_pairs={{0,48},{16,32},{32,16},{48,0},{64,112},{80,96},{96,80},{112,64},{1... | collective-permute-start | bytes 393224 | tf_op jit(solution)/shard_map/ppermute | solution.py:11
  17.9 2.7 %collective-permute-done.5 = bf16[64,1024]{1,0:T(8,128)(2,1)S(1)} collective-permute-done((bf16[64,1024]{1,0:T(8,128)(2,1)S(1)}, bf16[64,1024]{1,0:T(8,128)(2,1)S(1)}, u32[]{:S(2)}, u32[]{:S(2)}) %collective-permute-start.5) | collective-permute-done | bytes 131104 | tf_op jit(solution)/shard_map/ppermute | solution.py:11
  21.2 0.7 fusion.19
  23.7 1.1 %collective-permute-done.7 = f32[1,32,4992]{2,1,0:T(8,128)S(1)} collective-permute-done((f32[1,32,4992]{2,1,0:T(8,128)S(1)}, f32[1,32,4992]{2,1,0:T(8,128)S(1)}, u32[]{:S(2)}, u32[]{:S(2)}) %collective-permute-start.7) | collective-permute-done | bytes 639008 | tf_op jit(solution)/shard_map/ppermute | solution.py:11
  25.3 2.6 %collective-permute-start.9 = (bf16[2,8,4992]{2,1,0:T(8,128)(2,1)S(1)}, bf16[2,8,4992]{2,1,0:T(8,128)(2,1)S(1)}, u32[]{:S(2)}, u32[]{:S(2)}) collective-permute-start(bf16[2,8,4992]{2,1,0:T(8,128)(2,1)S(1)} %get-tuple-element.39), channel_id=1, source_target_pairs={{0,8},{1,9},{2,10},{3,11},{4,12},{5,13},{6,14},{7,15},{8,0},{9,1},... | collective-permute-start | bytes 479240 | tf_op jit(solution)/shard_map/ppermute | solution.py:11
  27.9 1.3 %collective-permute-start.8 = (bf16[2,8,4992]{2,1,0:T(8,128)(2,1)S(1)}, bf16[2,8,4992]{2,1,0:T(8,128)(2,1)S(1)}, u32[]{:S(2)}, u32[]{:S(2)}) collective-permute-start(bf16[2,8,4992]{2,1,0:T(8,128)(2,1)S(1)} %get-tuple-element.40), channel_id=1, source_target_pairs={{0,4},{1,5},{2,6},{3,7},{4,0},{5,1},{6,2},{7,3},{8,12},{9,13},{10,... | collective-permute-start | bytes 479240 | tf_op jit(solution)/shard_map/ppermute | solution.py:11
  29.8 2.6 %collective-permute-start.15 = (bf16[2,8,4992]{2,1,0:T(8,128)(2,1)S(1)}, bf16[2,8,4992]{2,1,0:T(8,128)(2,1)S(1)}, u32[]{:S(2)}, u32[]{:S(2)}) collective-permute-start(bf16[2,8,4992]{2,1,0:T(8,128)(2,1)S(1)} %get-tuple-element.42), channel_id=1, source_target_pairs={{0,8},{1,9},{2,10},{3,11},{4,12},{5,13},{6,14},{7,15},{8,0},{9,1},... | collective-permute-start | bytes 479240 | tf_op jit(solution)/shard_map/ppermute | solution.py:11
  32.4 4.9 %collective-permute-done.10 = bf16[2,8,4992]{2,1,0:T(8,128)(2,1)S(1)} collective-permute-done((bf16[2,8,4992]{2,1,0:T(8,128)(2,1)S(1)}, bf16[2,8,4992]{2,1,0:T(8,128)(2,1)S(1)}, u32[]{:S(2)}, u32[]{:S(2)}) %collective-permute-start.10) | collective-permute-done | bytes 159776 | tf_op jit(solution)/shard_map/ppermute | solution.py:11
  37.7 4.8 %collective-permute-start.12 = (bf16[2,8,4992]{2,1,0:T(8,128)(2,1)S(1)}, bf16[2,8,4992]{2,1,0:T(8,128)(2,1)S(1)}, u32[]{:S(2)}, u32[]{:S(2)}) collective-permute-start(bf16[2,8,4992]{2,1,0:T(8,128)(2,1)S(1)} %get-tuple-element.34), channel_id=1, source_target_pairs={{0,2},{1,3},{2,0},{3,1},{4,6},{5,7},{6,4},{7,5},{8,10},{9,11},{10,... | collective-permute-start | bytes 479240 | tf_op jit(solution)/shard_map/ppermute | solution.py:11
  43.5 4.7 %collective-permute-start.19 = (bf16[2,8,4992]{2,1,0:T(8,128)(2,1)S(1)}, bf16[2,8,4992]{2,1,0:T(8,128)(2,1)S(1)}, u32[]{:S(2)}, u32[]{:S(2)}) collective-permute-start(bf16[2,8,4992]{2,1,0:T(8,128)(2,1)S(1)} %fusion.41), channel_id=1, source_target_pairs={{0,2},{1,3},{2,0},{3,1},{4,6},{5,7},{6,4},{7,5},{8,10},{9,11},{10,... | collective-permute-start | bytes 479240 | tf_op jit(solution)/shard_map/ppermute | solution.py:11
  48.8 1.4 %collective-permute-start.17 = (bf16[2,8,4992]{2,1,0:T(8,128)(2,1)S(1)}, bf16[2,8,4992]{2,1,0:T(8,128)(2,1)S(1)}, u32[]{:S(2)}, u32[]{:S(2)}) collective-permute-start(bf16[2,8,4992]{2,1,0:T(8,128)(2,1)S(1)} %get-tuple-element.53), channel_id=1, source_target_pairs={{0,4},{1,5},{2,6},{3,7},{4,0},{5,1},{6,2},{7,3},{8,12},{9,13},{10,... | collective-permute-start | bytes 479240 | tf_op jit(solution)/shard_map/ppermute | solution.py:11
  50.1 2.9 %collective-permute-start.16 = (bf16[2,8,4992]{2,1,0:T(8,128)(2,1)S(1)}, bf16[2,8,4992]{2,1,0:T(8,128)(2,1)S(1)}, u32[]{:S(2)}, u32[]{:S(2)}) collective-permute-start(bf16[2,8,4992]{2,1,0:T(8,128)(2,1)S(1)} %get-tuple-element.53), channel_id=1, source_target_pairs={{0,8},{1,9},{2,10},{3,11},{4,12},{5,13},{6,14},{7,15},{8,0},{9,1},... | collective-permute-start | bytes 479240 | tf_op jit(solution)/shard_map/ppermute | solution.py:11
  53.1 4.6 %collective-permute-done.19 = bf16[2,8,4992]{2,1,0:T(8,128)(2,1)S(1)} collective-permute-done((bf16[2,8,4992]{2,1,0:T(8,128)(2,1)S(1)}, bf16[2,8,4992]{2,1,0:T(8,128)(2,1)S(1)}, u32[]{:S(2)}, u32[]{:S(2)}) %collective-permute-start.19) | collective-permute-done | bytes 159776 | tf_op jit(solution)/shard_map/ppermute | solution.py:11
  58.3 0.8 collective-permute-start.23
  59.1 3.6 %collective-permute-start.22 = (bf16[2,8,4992]{2,1,0:T(8,128)(2,1)S(1)}, bf16[2,8,4992]{2,1,0:T(8,128)(2,1)S(1)}, u32[]{:S(2)}, u32[]{:S(2)}) collective-permute-start(bf16[2,8,4992]{2,1,0:T(8,128)(2,1)S(1)} %get-tuple-element.54), channel_id=1, source_target_pairs={{0,8},{1,9},{2,10},{3,11},{4,12},{5,13},{6,14},{7,15},{8,0},{9,1},... | collective-permute-start | bytes 479240 | tf_op jit(solution)/shard_map/ppermute | solution.py:11
  62.9 3.3 %collective-permute-done.24 = bf16[2,8,4992]{2,1,0:T(8,128)(2,1)S(1)} collective-permute-done((bf16[2,8,4992]{2,1,0:T(8,128)(2,1)S(1)}, bf16[2,8,4992]{2,1,0:T(8,128)(2,1)S(1)}, u32[]{:S(2)}, u32[]{:S(2)}) %collective-permute-start.24) | collective-permute-done | bytes 159776 | tf_op jit(solution)/shard_map/ppermute | solution.py:11
  66.2 2.4 %collective-permute-done.22 = bf16[2,8,4992]{2,1,0:T(8,128)(2,1)S(1)} collective-permute-done((bf16[2,8,4992]{2,1,0:T(8,128)(2,1)S(1)}, bf16[2,8,4992]{2,1,0:T(8,128)(2,1)S(1)}, u32[]{:S(2)}, u32[]{:S(2)}) %collective-permute-start.22) | collective-permute-done | bytes 159776 | tf_op jit(solution)/shard_map/ppermute | solution.py:11
  68.9 0.7 fusion.7
  69.6 0.7 convolution_add_fusion.1
  72.6 1.8 %collective-permute-start.26 = (f32[64,512]{1,0:T(8,128)S(1)}, f32[64,512]{1,0:T(8,128)S(1)}, u32[]{:S(2)}, u32[]{:S(2)}) collective-permute-start(f32[64,512]{1,0:T(8,128)S(1)} %get-tuple-element.50), channel_id=1, source_target_pairs={{0,48},{16,32},{32,16},{48,0},{64,112},{80,96},{96,80},{112,64},{1... | collective-permute-start | bytes 393224 | tf_op jit(solution)/shard_map/ppermute | solution.py:11
  74.4 1.2 %collective-permute-start.27 = (f32[64,512]{1,0:T(8,128)S(1)}, f32[64,512]{1,0:T(8,128)S(1)}, u32[]{:S(2)}, u32[]{:S(2)}) collective-permute-start(f32[64,512]{1,0:T(8,128)S(1)} %get-tuple-element.51), channel_id=1, source_target_pairs={{0,16},{16,0},{32,48},{48,32},{64,80},{80,64},{96,112},{112,96},{1... | collective-permute-start | bytes 393224 | tf_op jit(solution)/shard_map/ppermute | solution.py:11
  75.6 1.8 %multiply_convert_fusion = bf16[1664,512]{1,0:T(8,128)(2,1)} fusion(bf16[256,4992]{1,0:T(8,128)(2,1)S(1)} %pad_maximum_fusion.2, bf16[256,1024]{1,0:T(8,128)(2,1)S(1)} %pad_maximum_fusion.6), kind=kOutput, calls=%fused_computation | convolution fusion | flops 437911552 | bytes 2818048 | tf_op jit(solution)/shard_map/dot_general | solution.py:47
  77.4 1.9 %multiply_convert_fusion.1 = bf16[512,1664]{1,0:T(8,128)(2,1)} fusion(bf16[256,4992]{1,0:T(8,128)(2,1)S(1)} %pad_maximum_fusion.2, bf16[256,1024]{1,0:T(8,128)(2,1)S(1)} %pad_maximum_fusion.6), kind=kOutput, calls=%fused_computation.1 | convolution fusion | flops 437911552 | bytes 2818048 | tf_op jit(solution)/shard_map/dot_general | solution.py:47
  79.3 1.3 %collective-permute-done.26 = f32[64,512]{1,0:T(8,128)S(1)} collective-permute-done((f32[64,512]{1,0:T(8,128)S(1)}, f32[64,512]{1,0:T(8,128)S(1)}, u32[]{:S(2)}, u32[]{:S(2)}) %collective-permute-start.26) | collective-permute-done | bytes 131104 | tf_op jit(solution)/shard_map/ppermute | solution.py:11
  80.8 1.8 %collective-permute-start.28 = (f32[16,512]{1,0:T(8,128)S(1)}, f32[16,512]{1,0:T(8,128)S(1)}, u32[]{:S(2)}, u32[]{:S(2)}) collective-permute-start(f32[16,512]{1,0:T(8,128)S(1)} %get-tuple-element.56), channel_id=1, source_target_pairs={{0,192},{16,208},{32,224},{48,240},{64,128},{80,144},{96,160},{112... | collective-permute-start | bytes 98312 | tf_op jit(solution)/shard_map/ppermute | solution.py:11
  82.6 2.7 %collective-permute-start.29 = (f32[16,512]{1,0:T(8,128)S(1)}, f32[16,512]{1,0:T(8,128)S(1)}, u32[]{:S(2)}, u32[]{:S(2)}) collective-permute-start(f32[16,512]{1,0:T(8,128)S(1)} %get-tuple-element.58), channel_id=1, source_target_pairs={{0,64},{16,80},{32,96},{48,112},{64,0},{80,16},{96,32},{112,48},{1... | collective-permute-start | bytes 98312 | tf_op jit(solution)/shard_map/ppermute | solution.py:11
  85.3 1.9 %multiply_convert_fusion.2 = bf16[512,1664]{1,0:T(8,128)(2,1)} fusion(bf16[256,4992]{1,0:T(8,128)(2,1)S(1)} %pad_maximum_fusion.2, bf16[256,1024]{1,0:T(8,128)(2,1)S(1)} %pad_maximum_fusion.6), kind=kOutput, calls=%fused_computation.2 | convolution fusion | flops 437911552 | bytes 2818048 | tf_op jit(solution)/shard_map/dot_general | solution.py:47
  (106 shorter events, 13.0 us)
Async XLA Ops:
  0.6 16.0 %copy-start = (bf16[512,1664]{1,0:T(8,128)(2,1)S(1)}, bf16[512,1664]{1,0:T(8,128)(2,1)}, u32[]{:S(2)}) copy-start(bf16[512,1664]{1,0:T(8,128)(2,1)} %param.6) | copy-start | bytes 5111812
  1.5 6.7 %collective-permute-start.2 = (bf16[16,1024]{1,0:T(8,128)(2,1)S(1)}, bf16[16,1024]{1,0:T(8,128)(2,1)S(1)}, u32[]{:S(2)}, u32[]{:S(2)}) collective-permute-start(bf16[16,1024]{1,0:T(8,128)(2,1)S(1)} %pad_add_fusion), channel_id=1, source_target_pairs={{0,192},{16,208},{32,224},{48,240},{64,128},{80,144},{96,160},{112... | collective-permute-start | bytes 98312 | tf_op jit(solution)/shard_map/ppermute | solution.py:11
  6.1 4.8 %collective-permute-start.1 = (bf16[16,1024]{1,0:T(8,128)(2,1)S(1)}, bf16[16,1024]{1,0:T(8,128)(2,1)S(1)}, u32[]{:S(2)}, u32[]{:S(2)}) collective-permute-start(bf16[16,1024]{1,0:T(8,128)(2,1)S(1)} %pad_add_fusion), channel_id=1, source_target_pairs={{0,128},{16,144},{32,160},{48,176},{64,192},{80,208},{96,224},{112... | collective-permute-start | bytes 98312 | tf_op jit(solution)/shard_map/ppermute | solution.py:11
  6.1 4.8 %collective-permute-start = (bf16[16,1024]{1,0:T(8,128)(2,1)S(1)}, bf16[16,1024]{1,0:T(8,128)(2,1)S(1)}, u32[]{:S(2)}, u32[]{:S(2)}) collective-permute-start(bf16[16,1024]{1,0:T(8,128)(2,1)S(1)} %pad_add_fusion), channel_id=1, source_target_pairs={{0,64},{16,80},{32,96},{48,112},{64,0},{80,16},{96,32},{112,48},{1... | collective-permute-start | bytes 98312 | tf_op jit(solution)/shard_map/ppermute | solution.py:11
  11.3 6.7 %collective-permute-start.6 = (bf16[64,1024]{1,0:T(8,128)(2,1)S(1)}, bf16[64,1024]{1,0:T(8,128)(2,1)S(1)}, u32[]{:S(2)}, u32[]{:S(2)}) collective-permute-start(bf16[64,1024]{1,0:T(8,128)(2,1)S(1)} %fusion.28), channel_id=1, source_target_pairs={{0,32},{16,48},{32,0},{48,16},{64,96},{80,112},{96,64},{112,80},{1... | collective-permute-start | bytes 393224 | tf_op jit(solution)/shard_map/ppermute | solution.py:11
  14.4 6.3 %collective-permute-start.5 = (bf16[64,1024]{1,0:T(8,128)(2,1)S(1)}, bf16[64,1024]{1,0:T(8,128)(2,1)S(1)}, u32[]{:S(2)}, u32[]{:S(2)}) collective-permute-start(bf16[64,1024]{1,0:T(8,128)(2,1)S(1)} %fusion.28), channel_id=1, source_target_pairs={{0,48},{16,32},{32,16},{48,0},{64,112},{80,96},{96,80},{112,64},{1... | collective-permute-start | bytes 393224 | tf_op jit(solution)/shard_map/ppermute | solution.py:11
  15.5 5.1 %collective-permute-start.4 = (bf16[64,1024]{1,0:T(8,128)(2,1)S(1)}, bf16[64,1024]{1,0:T(8,128)(2,1)S(1)}, u32[]{:S(2)}, u32[]{:S(2)}) collective-permute-start(bf16[64,1024]{1,0:T(8,128)(2,1)S(1)} %fusion.28), channel_id=1, source_target_pairs={{0,16},{16,0},{32,48},{48,32},{64,80},{80,64},{96,112},{112,96},{1... | collective-permute-start | bytes 393224 | tf_op jit(solution)/shard_map/ppermute | solution.py:11
  17.2 6.5 %collective-permute-start.3 = (f32[1,32,4992]{2,1,0:T(8,128)S(1)}, f32[1,32,4992]{2,1,0:T(8,128)S(1)}, u32[]{:S(2)}, u32[]{:S(2)}) collective-permute-start(f32[1,32,4992]{2,1,0:T(8,128)S(1)} %slice.261), channel_id=1, source_target_pairs={{0,1},{1,0},{2,3},{3,2},{4,5},{5,4},{6,7},{7,6},{8,9},{9,8},{10,11... | collective-permute-start | bytes 1916936 | tf_op jit(solution)/shard_map/ppermute | solution.py:11
  22.6 2.2 %collective-permute-start.7 = (f32[1,32,4992]{2,1,0:T(8,128)S(1)}, f32[1,32,4992]{2,1,0:T(8,128)S(1)}, u32[]{:S(2)}, u32[]{:S(2)}) collective-permute-start(f32[1,32,4992]{2,1,0:T(8,128)S(1)} %slice.265), channel_id=1, source_target_pairs={{0,1},{1,0},{2,3},{3,2},{4,5},{5,4},{6,7},{7,6},{8,9},{9,8},{10,11... | collective-permute-start | bytes 1916936 | tf_op jit(solution)/shard_map/ppermute | solution.py:11
  23.0 6.2 %collective-permute-start.11 = (f32[2,32,4992]{2,1,0:T(8,128)S(1)}, f32[2,32,4992]{2,1,0:T(8,128)S(1)}, u32[]{:S(2)}, u32[]{:S(2)}) collective-permute-start(f32[2,32,4992]{2,1,0:T(8,128)S(1)} %slice.272), channel_id=1, source_target_pairs={{0,1},{1,0},{2,3},{3,2},{4,5},{5,4},{6,7},{7,6},{8,9},{9,8},{10,11... | collective-permute-start | bytes 3833864 | tf_op jit(solution)/shard_map/ppermute | solution.py:11
  25.0 12.3 %collective-permute-start.10 = (bf16[2,8,4992]{2,1,0:T(8,128)(2,1)S(1)}, bf16[2,8,4992]{2,1,0:T(8,128)(2,1)S(1)}, u32[]{:S(2)}, u32[]{:S(2)}) collective-permute-start(bf16[2,8,4992]{2,1,0:T(8,128)(2,1)S(1)} %get-tuple-element.38), channel_id=1, source_target_pairs={{0,12},{1,13},{2,14},{3,15},{4,8},{5,9},{6,10},{7,11},{8,4},{9,5},... | collective-permute-start | bytes 479240 | tf_op jit(solution)/shard_map/ppermute | solution.py:11
  25.3 12.0 %collective-permute-start.9 = (bf16[2,8,4992]{2,1,0:T(8,128)(2,1)S(1)}, bf16[2,8,4992]{2,1,0:T(8,128)(2,1)S(1)}, u32[]{:S(2)}, u32[]{:S(2)}) collective-permute-start(bf16[2,8,4992]{2,1,0:T(8,128)(2,1)S(1)} %get-tuple-element.39), channel_id=1, source_target_pairs={{0,8},{1,9},{2,10},{3,11},{4,12},{5,13},{6,14},{7,15},{8,0},{9,1},... | collective-permute-start | bytes 479240 | tf_op jit(solution)/shard_map/ppermute | solution.py:11
  27.9 9.7 %collective-permute-start.8 = (bf16[2,8,4992]{2,1,0:T(8,128)(2,1)S(1)}, bf16[2,8,4992]{2,1,0:T(8,128)(2,1)S(1)}, u32[]{:S(2)}, u32[]{:S(2)}) collective-permute-start(bf16[2,8,4992]{2,1,0:T(8,128)(2,1)S(1)} %get-tuple-element.40), channel_id=1, source_target_pairs={{0,4},{1,5},{2,6},{3,7},{4,0},{5,1},{6,2},{7,3},{8,12},{9,13},{10,... | collective-permute-start | bytes 479240 | tf_op jit(solution)/shard_map/ppermute | solution.py:11
  29.5 13.3 %collective-permute-start.13 = (bf16[2,8,4992]{2,1,0:T(8,128)(2,1)S(1)}, bf16[2,8,4992]{2,1,0:T(8,128)(2,1)S(1)}, u32[]{:S(2)}, u32[]{:S(2)}) collective-permute-start(bf16[2,8,4992]{2,1,0:T(8,128)(2,1)S(1)} %get-tuple-element.41), channel_id=1, source_target_pairs={{0,12},{1,13},{2,14},{3,15},{4,8},{5,9},{6,10},{7,11},{8,4},{9,5},... | collective-permute-start | bytes 479240 | tf_op jit(solution)/shard_map/ppermute | solution.py:11
  29.8 13.0 %collective-permute-start.15 = (bf16[2,8,4992]{2,1,0:T(8,128)(2,1)S(1)}, bf16[2,8,4992]{2,1,0:T(8,128)(2,1)S(1)}, u32[]{:S(2)}, u32[]{:S(2)}) collective-permute-start(bf16[2,8,4992]{2,1,0:T(8,128)(2,1)S(1)} %get-tuple-element.42), channel_id=1, source_target_pairs={{0,8},{1,9},{2,10},{3,11},{4,12},{5,13},{6,14},{7,15},{8,0},{9,1},... | collective-permute-start | bytes 479240 | tf_op jit(solution)/shard_map/ppermute | solution.py:11
  37.3 6.1 %collective-permute-start.14 = (bf16[2,8,4992]{2,1,0:T(8,128)(2,1)S(1)}, bf16[2,8,4992]{2,1,0:T(8,128)(2,1)S(1)}, u32[]{:S(2)}, u32[]{:S(2)}) collective-permute-start(bf16[2,8,4992]{2,1,0:T(8,128)(2,1)S(1)} %get-tuple-element.43), channel_id=1, source_target_pairs={{0,4},{1,5},{2,6},{3,7},{4,0},{5,1},{6,2},{7,3},{8,12},{9,13},{10,... | collective-permute-start | bytes 479240 | tf_op jit(solution)/shard_map/ppermute | solution.py:11
  37.7 10.5 %collective-permute-start.12 = (bf16[2,8,4992]{2,1,0:T(8,128)(2,1)S(1)}, bf16[2,8,4992]{2,1,0:T(8,128)(2,1)S(1)}, u32[]{:S(2)}, u32[]{:S(2)}) collective-permute-start(bf16[2,8,4992]{2,1,0:T(8,128)(2,1)S(1)} %get-tuple-element.34), channel_id=1, source_target_pairs={{0,2},{1,3},{2,0},{3,1},{4,6},{5,7},{6,4},{7,5},{8,10},{9,11},{10,... | collective-permute-start | bytes 479240 | tf_op jit(solution)/shard_map/ppermute | solution.py:11
  43.5 14.2 %collective-permute-start.19 = (bf16[2,8,4992]{2,1,0:T(8,128)(2,1)S(1)}, bf16[2,8,4992]{2,1,0:T(8,128)(2,1)S(1)}, u32[]{:S(2)}, u32[]{:S(2)}) collective-permute-start(bf16[2,8,4992]{2,1,0:T(8,128)(2,1)S(1)} %fusion.41), channel_id=1, source_target_pairs={{0,2},{1,3},{2,0},{3,1},{4,6},{5,7},{6,4},{7,5},{8,10},{9,11},{10,... | collective-permute-start | bytes 479240 | tf_op jit(solution)/shard_map/ppermute | solution.py:11
  48.3 10.8 %collective-permute-start.18 = (bf16[2,8,4992]{2,1,0:T(8,128)(2,1)S(1)}, bf16[2,8,4992]{2,1,0:T(8,128)(2,1)S(1)}, u32[]{:S(2)}, u32[]{:S(2)}) collective-permute-start(bf16[2,8,4992]{2,1,0:T(8,128)(2,1)S(1)} %get-tuple-element.53), channel_id=1, source_target_pairs={{0,12},{1,13},{2,14},{3,15},{4,8},{5,9},{6,10},{7,11},{8,4},{9,5},... | collective-permute-start | bytes 479240 | tf_op jit(solution)/shard_map/ppermute | solution.py:11
  48.8 13.9 %collective-permute-start.17 = (bf16[2,8,4992]{2,1,0:T(8,128)(2,1)S(1)}, bf16[2,8,4992]{2,1,0:T(8,128)(2,1)S(1)}, u32[]{:S(2)}, u32[]{:S(2)}) collective-permute-start(bf16[2,8,4992]{2,1,0:T(8,128)(2,1)S(1)} %get-tuple-element.53), channel_id=1, source_target_pairs={{0,4},{1,5},{2,6},{3,7},{4,0},{5,1},{6,2},{7,3},{8,12},{9,13},{10,... | collective-permute-start | bytes 479240 | tf_op jit(solution)/shard_map/ppermute | solution.py:11
  50.1 12.5 %collective-permute-start.16 = (bf16[2,8,4992]{2,1,0:T(8,128)(2,1)S(1)}, bf16[2,8,4992]{2,1,0:T(8,128)(2,1)S(1)}, u32[]{:S(2)}, u32[]{:S(2)}) collective-permute-start(bf16[2,8,4992]{2,1,0:T(8,128)(2,1)S(1)} %get-tuple-element.53), channel_id=1, source_target_pairs={{0,8},{1,9},{2,10},{3,11},{4,12},{5,13},{6,14},{7,15},{8,0},{9,1},... | collective-permute-start | bytes 479240 | tf_op jit(solution)/shard_map/ppermute | solution.py:11
  57.9 8.3 %collective-permute-start.24 = (bf16[2,8,4992]{2,1,0:T(8,128)(2,1)S(1)}, bf16[2,8,4992]{2,1,0:T(8,128)(2,1)S(1)}, u32[]{:S(2)}, u32[]{:S(2)}) collective-permute-start(bf16[2,8,4992]{2,1,0:T(8,128)(2,1)S(1)} %get-tuple-element.54), channel_id=1, source_target_pairs={{0,12},{1,13},{2,14},{3,15},{4,8},{5,9},{6,10},{7,11},{8,4},{9,5},... | collective-permute-start | bytes 479240 | tf_op jit(solution)/shard_map/ppermute | solution.py:11
  58.3 7.9 %collective-permute-start.23 = (bf16[2,8,4992]{2,1,0:T(8,128)(2,1)S(1)}, bf16[2,8,4992]{2,1,0:T(8,128)(2,1)S(1)}, u32[]{:S(2)}, u32[]{:S(2)}) collective-permute-start(bf16[2,8,4992]{2,1,0:T(8,128)(2,1)S(1)} %get-tuple-element.54), channel_id=1, source_target_pairs={{0,4},{1,5},{2,6},{3,7},{4,0},{5,1},{6,2},{7,3},{8,12},{9,13},{10,... | collective-permute-start | bytes 479240 | tf_op jit(solution)/shard_map/ppermute | solution.py:11
  59.1 9.5 %collective-permute-start.22 = (bf16[2,8,4992]{2,1,0:T(8,128)(2,1)S(1)}, bf16[2,8,4992]{2,1,0:T(8,128)(2,1)S(1)}, u32[]{:S(2)}, u32[]{:S(2)}) collective-permute-start(bf16[2,8,4992]{2,1,0:T(8,128)(2,1)S(1)} %get-tuple-element.54), channel_id=1, source_target_pairs={{0,8},{1,9},{2,10},{3,11},{4,12},{5,13},{6,14},{7,15},{8,0},{9,1},... | collective-permute-start | bytes 479240 | tf_op jit(solution)/shard_map/ppermute | solution.py:11
  62.8 6.0 %collective-permute-start.20 = (bf16[2,32,4992]{2,1,0:T(8,128)(2,1)S(1)}, bf16[2,32,4992]{2,1,0:T(8,128)(2,1)S(1)}, u32[]{:S(2)}, u32[]{:S(2)}) collective-permute-start(bf16[2,32,4992]{2,1,0:T(8,128)(2,1)S(1)} %pad_maximum_fusion.4), channel_id=1, source_target_pairs={{0,1},{1,0},{2,3},{3,2},{4,5},{5,4},{6,7},{7,6},{8,9},{9,8},{10,11... | collective-permute-start | bytes 1916936 | tf_op jit(solution)/shard_map/ppermute | solution.py:11
  68.7 2.3 %collective-permute-start.25 = (bf16[2,32,4992]{2,1,0:T(8,128)(2,1)S(1)}, bf16[2,32,4992]{2,1,0:T(8,128)(2,1)S(1)}, u32[]{:S(2)}, u32[]{:S(2)}) collective-permute-start(bf16[2,32,4992]{2,1,0:T(8,128)(2,1)S(1)} %pad_maximum_fusion.5), channel_id=1, source_target_pairs={{0,1},{1,0},{2,3},{3,2},{4,5},{5,4},{6,7},{7,6},{8,9},{9,8},{10,11... | collective-permute-start | bytes 1916936 | tf_op jit(solution)/shard_map/ppermute | solution.py:11
  70.3 9.0 %collective-permute-start.21 = (f32[64,512]{1,0:T(8,128)S(1)}, f32[64,512]{1,0:T(8,128)S(1)}, u32[]{:S(2)}, u32[]{:S(2)}) collective-permute-start(f32[64,512]{1,0:T(8,128)S(1)} %slice.286), channel_id=1, source_target_pairs={{0,32},{16,48},{32,0},{48,16},{64,96},{80,112},{96,64},{112,80},{1... | collective-permute-start | bytes 393224 | tf_op jit(solution)/shard_map/ppermute | solution.py:11
  72.6 8.0 %collective-permute-start.26 = (f32[64,512]{1,0:T(8,128)S(1)}, f32[64,512]{1,0:T(8,128)S(1)}, u32[]{:S(2)}, u32[]{:S(2)}) collective-permute-start(f32[64,512]{1,0:T(8,128)S(1)} %get-tuple-element.50), channel_id=1, source_target_pairs={{0,48},{16,32},{32,16},{48,0},{64,112},{80,96},{96,80},{112,64},{1... | collective-permute-start | bytes 393224 | tf_op jit(solution)/shard_map/ppermute | solution.py:11
  74.4 6.2 %collective-permute-start.27 = (f32[64,512]{1,0:T(8,128)S(1)}, f32[64,512]{1,0:T(8,128)S(1)}, u32[]{:S(2)}, u32[]{:S(2)}) collective-permute-start(f32[64,512]{1,0:T(8,128)S(1)} %get-tuple-element.51), channel_id=1, source_target_pairs={{0,16},{16,0},{32,48},{48,32},{64,80},{80,64},{96,112},{112,96},{1... | collective-permute-start | bytes 393224 | tf_op jit(solution)/shard_map/ppermute | solution.py:11
  80.8 6.4 %collective-permute-start.28 = (f32[16,512]{1,0:T(8,128)S(1)}, f32[16,512]{1,0:T(8,128)S(1)}, u32[]{:S(2)}, u32[]{:S(2)}) collective-permute-start(f32[16,512]{1,0:T(8,128)S(1)} %get-tuple-element.56), channel_id=1, source_target_pairs={{0,192},{16,208},{32,224},{48,240},{64,128},{80,144},{96,160},{112... | collective-permute-start | bytes 98312 | tf_op jit(solution)/shard_map/ppermute | solution.py:11
  82.6 5.0 %collective-permute-start.30 = (f32[16,512]{1,0:T(8,128)S(1)}, f32[16,512]{1,0:T(8,128)S(1)}, u32[]{:S(2)}, u32[]{:S(2)}) collective-permute-start(f32[16,512]{1,0:T(8,128)S(1)} %get-tuple-element.57), channel_id=1, source_target_pairs={{0,128},{16,144},{32,160},{48,176},{64,192},{80,208},{96,224},{112... | collective-permute-start | bytes 98312 | tf_op jit(solution)/shard_map/ppermute | solution.py:11
  82.6 5.0 %collective-permute-start.29 = (f32[16,512]{1,0:T(8,128)S(1)}, f32[16,512]{1,0:T(8,128)S(1)}, u32[]{:S(2)}, u32[]{:S(2)}) collective-permute-start(f32[16,512]{1,0:T(8,128)S(1)} %get-tuple-element.58), channel_id=1, source_target_pairs={{0,64},{16,80},{32,96},{48,112},{64,0},{80,16},{96,32},{112,48},{1... | collective-permute-start | bytes 98312 | tf_op jit(solution)/shard_map/ppermute | solution.py:11
  (2 other events, 9.3 us)

commit v3 on v2

--- a/solution.py
+++ b/solution.py
@@ -148,7 +148,7 @@
     input_grad = total.astype(BF16)
 
     panel = jnp.concatenate((own, near, rest[:128]), axis=0)
-    cots = after(jnp.concatenate(fulls, axis=0), back)
+    cots = jnp.concatenate(after(fulls, back), axis=0)
     factor = F32(panel.shape[0]) ** (-0.5)
     token, cot = panel[:, :depth], panel[:, depth:]
     rows = ((0,), (0,))

time: 88.4 us -> 88.3 us (level)
  transfers between devices with their start and end apart: 31 -> 31, of which waited for: 14 -> 14; matrix products, arithmetic and copies ran while one was open for 15% -> 16% of each run, Pallas kernels for 0% -> 0%
where the time goes in v3:
time: 88.3 us; the launch traced here: 88.1 us
  starting transfers between devices  44.7 us (51%)
  waiting for transfers between devices  26.6 us (30%)
  matrix products  11.6 us (13%)
  other arithmetic  3.17 us (4%)
  between operations  1.16 us (1%)
  local copies, waits for them, and re-layouts  0.89 us (1%)
    ppermute x31, starting transfers between devices, swapped(): return lambda a: lax.ppermute(a, axis, [(i, i ^ mask) for i in range(16)])  44.7 us
    ppermute x31, waiting for transfers between devices, swapped(): return lambda a: lax.ppermute(a, axis, [(i, i ^ mask) for i in range(16)])  26.6 us
    dot_general x13, matrix products, dot(): lax.dot_general(left, right, (dims, ((), ())), preferred_element_type=F32)  11.6 us
  transfers between devices with their start and end apart: 31, of which 14 were waited for; matrix products, arithmetic and copies ran while one was open for 16% of the time, Pallas kernels for 0%

profile of v3, /device:TPU:24, one launch (start us, length us, event | category | flops | bytes accessed | tf_op | source)
XLA Modules:
  0.0 88.1 jit_solution(51229610229866077)
XLA Ops:
  0.6 0.9 pad_add_fusion
  1.5 4.6 %collective-permute-start.2 = (bf16[16,1024]{1,0:T(8,128)(2,1)S(1)}, bf16[16,1024]{1,0:T(8,128)(2,1)S(1)}, u32[]{:S(2)}, u32[]{:S(2)}) collective-permute-start(bf16[16,1024]{1,0:T(8,128)(2,1)S(1)} %pad_add_fusion), channel_id=1, source_target_pairs={{0,192},{16,208},{32,224},{48,240},{64,128},{80,144},{96,160},{112... | collective-permute-start | bytes 98312 | tf_op jit(solution)/shard_map/ppermute | solution.py:11
  6.7 1.5 %collective-permute-done.2 = bf16[16,1024]{1,0:T(8,128)(2,1)S(1)} collective-permute-done((bf16[16,1024]{1,0:T(8,128)(2,1)S(1)}, bf16[16,1024]{1,0:T(8,128)(2,1)S(1)}, u32[]{:S(2)}, u32[]{:S(2)}) %collective-permute-start.2) | collective-permute-done | bytes 32800 | tf_op jit(solution)/shard_map/ppermute | solution.py:11
  8.2 2.7 %collective-permute-done.1 = bf16[16,1024]{1,0:T(8,128)(2,1)S(1)} collective-permute-done((bf16[16,1024]{1,0:T(8,128)(2,1)S(1)}, bf16[16,1024]{1,0:T(8,128)(2,1)S(1)}, u32[]{:S(2)}, u32[]{:S(2)}) %collective-permute-start.1) | collective-permute-done | bytes 32800 | tf_op jit(solution)/shard_map/ppermute | solution.py:11
  11.3 3.1 %collective-permute-start.6 = (bf16[64,1024]{1,0:T(8,128)(2,1)S(1)}, bf16[64,1024]{1,0:T(8,128)(2,1)S(1)}, u32[]{:S(2)}, u32[]{:S(2)}) collective-permute-start(bf16[64,1024]{1,0:T(8,128)(2,1)S(1)} %fusion.28), channel_id=1, source_target_pairs={{0,32},{16,48},{32,0},{48,16},{64,96},{80,112},{96,64},{112,80},{1... | collective-permute-start | bytes 393224 | tf_op jit(solution)/shard_map/ppermute | solution.py:11
  14.4 1.1 %collective-permute-start.5 = (bf16[64,1024]{1,0:T(8,128)(2,1)S(1)}, bf16[64,1024]{1,0:T(8,128)(2,1)S(1)}, u32[]{:S(2)}, u32[]{:S(2)}) collective-permute-start(bf16[64,1024]{1,0:T(8,128)(2,1)S(1)} %fusion.28), channel_id=1, source_target_pairs={{0,48},{16,32},{32,16},{48,0},{64,112},{80,96},{96,80},{112,64},{1... | collective-permute-start | bytes 393224 | tf_op jit(solution)/shard_map/ppermute | solution.py:11
  17.9 2.7 %collective-permute-done.5 = bf16[64,1024]{1,0:T(8,128)(2,1)S(1)} collective-permute-done((bf16[64,1024]{1,0:T(8,128)(2,1)S(1)}, bf16[64,1024]{1,0:T(8,128)(2,1)S(1)}, u32[]{:S(2)}, u32[]{:S(2)}) %collective-permute-start.5) | collective-permute-done | bytes 131104 | tf_op jit(solution)/shard_map/ppermute | solution.py:11
  21.2 0.7 fusion.19
  23.7 1.1 %collective-permute-done.7 = f32[1,32,4992]{2,1,0:T(8,128)S(1)} collective-permute-done((f32[1,32,4992]{2,1,0:T(8,128)S(1)}, f32[1,32,4992]{2,1,0:T(8,128)S(1)}, u32[]{:S(2)}, u32[]{:S(2)}) %collective-permute-start.7) | collective-permute-done | bytes 639008 | tf_op jit(solution)/shard_map/ppermute | solution.py:11
  25.3 2.6 %collective-permute-start.9 = (bf16[2,8,4992]{2,1,0:T(8,128)(2,1)S(1)}, bf16[2,8,4992]{2,1,0:T(8,128)(2,1)S(1)}, u32[]{:S(2)}, u32[]{:S(2)}) collective-permute-start(bf16[2,8,4992]{2,1,0:T(8,128)(2,1)S(1)} %get-tuple-element.41), channel_id=1, source_target_pairs={{0,8},{1,9},{2,10},{3,11},{4,12},{5,13},{6,14},{7,15},{8,0},{9,1},... | collective-permute-start | bytes 479240 | tf_op jit(solution)/shard_map/ppermute | solution.py:11
  27.9 1.3 %collective-permute-start.8 = (bf16[2,8,4992]{2,1,0:T(8,128)(2,1)S(1)}, bf16[2,8,4992]{2,1,0:T(8,128)(2,1)S(1)}, u32[]{:S(2)}, u32[]{:S(2)}) collective-permute-start(bf16[2,8,4992]{2,1,0:T(8,128)(2,1)S(1)} %get-tuple-element.42), channel_id=1, source_target_pairs={{0,4},{1,5},{2,6},{3,7},{4,0},{5,1},{6,2},{7,3},{8,12},{9,13},{10,... | collective-permute-start | bytes 479240 | tf_op jit(solution)/shard_map/ppermute | solution.py:11
  29.7 2.6 %collective-permute-start.15 = (bf16[2,8,4992]{2,1,0:T(8,128)(2,1)S(1)}, bf16[2,8,4992]{2,1,0:T(8,128)(2,1)S(1)}, u32[]{:S(2)}, u32[]{:S(2)}) collective-permute-start(bf16[2,8,4992]{2,1,0:T(8,128)(2,1)S(1)} %get-tuple-element.44), channel_id=1, source_target_pairs={{0,8},{1,9},{2,10},{3,11},{4,12},{5,13},{6,14},{7,15},{8,0},{9,1},... | collective-permute-start | bytes 479240 | tf_op jit(solution)/shard_map/ppermute | solution.py:11
  32.3 5.0 %collective-permute-done.10 = bf16[2,8,4992]{2,1,0:T(8,128)(2,1)S(1)} collective-permute-done((bf16[2,8,4992]{2,1,0:T(8,128)(2,1)S(1)}, bf16[2,8,4992]{2,1,0:T(8,128)(2,1)S(1)}, u32[]{:S(2)}, u32[]{:S(2)}) %collective-permute-start.10) | collective-permute-done | bytes 159776 | tf_op jit(solution)/shard_map/ppermute | solution.py:11
  37.7 4.9 %collective-permute-start.12 = (bf16[2,8,4992]{2,1,0:T(8,128)(2,1)S(1)}, bf16[2,8,4992]{2,1,0:T(8,128)(2,1)S(1)}, u32[]{:S(2)}, u32[]{:S(2)}) collective-permute-start(bf16[2,8,4992]{2,1,0:T(8,128)(2,1)S(1)} %get-tuple-element.36), channel_id=1, source_target_pairs={{0,2},{1,3},{2,0},{3,1},{4,6},{5,7},{6,4},{7,5},{8,10},{9,11},{10,... | collective-permute-start | bytes 479240 | tf_op jit(solution)/shard_map/ppermute | solution.py:11
  43.5 4.7 %collective-permute-start.19 = (bf16[2,8,4992]{2,1,0:T(8,128)(2,1)S(1)}, bf16[2,8,4992]{2,1,0:T(8,128)(2,1)S(1)}, u32[]{:S(2)}, u32[]{:S(2)}) collective-permute-start(bf16[2,8,4992]{2,1,0:T(8,128)(2,1)S(1)} %fusion.41), channel_id=1, source_target_pairs={{0,2},{1,3},{2,0},{3,1},{4,6},{5,7},{6,4},{7,5},{8,10},{9,11},{10,... | collective-permute-start | bytes 479240 | tf_op jit(solution)/shard_map/ppermute | solution.py:11
  48.8 1.4 %collective-permute-start.17 = (bf16[2,8,4992]{2,1,0:T(8,128)(2,1)S(1)}, bf16[2,8,4992]{2,1,0:T(8,128)(2,1)S(1)}, u32[]{:S(2)}, u32[]{:S(2)}) collective-permute-start(bf16[2,8,4992]{2,1,0:T(8,128)(2,1)S(1)} %get-tuple-element.55), channel_id=1, source_target_pairs={{0,4},{1,5},{2,6},{3,7},{4,0},{5,1},{6,2},{7,3},{8,12},{9,13},{10,... | collective-permute-start | bytes 479240 | tf_op jit(solution)/shard_map/ppermute | solution.py:11
  50.2 2.9 %collective-permute-start.16 = (bf16[2,8,4992]{2,1,0:T(8,128)(2,1)S(1)}, bf16[2,8,4992]{2,1,0:T(8,128)(2,1)S(1)}, u32[]{:S(2)}, u32[]{:S(2)}) collective-permute-start(bf16[2,8,4992]{2,1,0:T(8,128)(2,1)S(1)} %get-tuple-element.55), channel_id=1, source_target_pairs={{0,8},{1,9},{2,10},{3,11},{4,12},{5,13},{6,14},{7,15},{8,0},{9,1},... | collective-permute-start | bytes 479240 | tf_op jit(solution)/shard_map/ppermute | solution.py:11
  53.1 4.6 %collective-permute-done.19 = bf16[2,8,4992]{2,1,0:T(8,128)(2,1)S(1)} collective-permute-done((bf16[2,8,4992]{2,1,0:T(8,128)(2,1)S(1)}, bf16[2,8,4992]{2,1,0:T(8,128)(2,1)S(1)}, u32[]{:S(2)}, u32[]{:S(2)}) %collective-permute-start.19) | collective-permute-done | bytes 159776 | tf_op jit(solution)/shard_map/ppermute | solution.py:11
  58.3 0.8 collective-permute-start.23
  59.1 3.6 %collective-permute-start.22 = (bf16[2,8,4992]{2,1,0:T(8,128)(2,1)S(1)}, bf16[2,8,4992]{2,1,0:T(8,128)(2,1)S(1)}, u32[]{:S(2)}, u32[]{:S(2)}) collective-permute-start(bf16[2,8,4992]{2,1,0:T(8,128)(2,1)S(1)} %get-tuple-element.56), channel_id=1, source_target_pairs={{0,8},{1,9},{2,10},{3,11},{4,12},{5,13},{6,14},{7,15},{8,0},{9,1},... | collective-permute-start | bytes 479240 | tf_op jit(solution)/shard_map/ppermute | solution.py:11
  62.9 3.3 %collective-permute-done.24 = bf16[2,8,4992]{2,1,0:T(8,128)(2,1)S(1)} collective-permute-done((bf16[2,8,4992]{2,1,0:T(8,128)(2,1)S(1)}, bf16[2,8,4992]{2,1,0:T(8,128)(2,1)S(1)}, u32[]{:S(2)}, u32[]{:S(2)}) %collective-permute-start.24) | collective-permute-done | bytes 159776 | tf_op jit(solution)/shard_map/ppermute | solution.py:11
  66.2 2.4 %collective-permute-done.22 = bf16[2,8,4992]{2,1,0:T(8,128)(2,1)S(1)} collective-permute-done((bf16[2,8,4992]{2,1,0:T(8,128)(2,1)S(1)}, bf16[2,8,4992]{2,1,0:T(8,128)(2,1)S(1)}, u32[]{:S(2)}, u32[]{:S(2)}) %collective-permute-start.22) | collective-permute-done | bytes 159776 | tf_op jit(solution)/shard_map/ppermute | solution.py:11
  69.6 0.7 convolution_add_fusion.1
  71.7 0.7 convolution_add_fusion
  72.4 1.8 %collective-permute-start.26 = (f32[64,512]{1,0:T(8,128)S(1)}, f32[64,512]{1,0:T(8,128)S(1)}, u32[]{:S(2)}, u32[]{:S(2)}) collective-permute-start(f32[64,512]{1,0:T(8,128)S(1)} %get-tuple-element.52), channel_id=1, source_target_pairs={{0,48},{16,32},{32,16},{48,0},{64,112},{80,96},{96,80},{112,64},{1... | collective-permute-start | bytes 393224 | tf_op jit(solution)/shard_map/ppermute | solution.py:11
  74.2 1.2 %collective-permute-start.27 = (f32[64,512]{1,0:T(8,128)S(1)}, f32[64,512]{1,0:T(8,128)S(1)}, u32[]{:S(2)}, u32[]{:S(2)}) collective-permute-start(f32[64,512]{1,0:T(8,128)S(1)} %get-tuple-element.53), channel_id=1, source_target_pairs={{0,16},{16,0},{32,48},{48,32},{64,80},{80,64},{96,112},{112,96},{1... | collective-permute-start | bytes 393224 | tf_op jit(solution)/shard_map/ppermute | solution.py:11
  75.7 1.8 %multiply_convert_fusion = bf16[1664,512]{1,0:T(8,128)(2,1)} fusion(bf16[256,4992]{1,0:T(8,128)(2,1)S(1)} %constant_dynamic-update-slice_fusion.13, bf16[256,1024]{1,0:T(8,128)(2,1)S(1)} %pad_maximum_fusion.5), kind=kOutput, calls=%fused_computation | convolution fusion | flops 437911552 | bytes 2818048 | tf_op jit(solution)/shard_map/dot_general | solution.py:47
  77.5 1.9 %multiply_convert_fusion.1 = bf16[512,1664]{1,0:T(8,128)(2,1)} fusion(bf16[256,4992]{1,0:T(8,128)(2,1)S(1)} %constant_dynamic-update-slice_fusion.13, bf16[256,1024]{1,0:T(8,128)(2,1)S(1)} %pad_maximum_fusion.5), kind=kOutput, calls=%fused_computation.1 | convolution fusion | flops 437911552 | bytes 2818048 | tf_op jit(solution)/shard_map/dot_general | solution.py:47
  79.4 1.2 %collective-permute-done.26 = f32[64,512]{1,0:T(8,128)S(1)} collective-permute-done((f32[64,512]{1,0:T(8,128)S(1)}, f32[64,512]{1,0:T(8,128)S(1)}, u32[]{:S(2)}, u32[]{:S(2)}) %collective-permute-start.26) | collective-permute-done | bytes 131104 | tf_op jit(solution)/shard_map/ppermute | solution.py:11
  80.8 1.7 %collective-permute-start.28 = (f32[16,512]{1,0:T(8,128)S(1)}, f32[16,512]{1,0:T(8,128)S(1)}, u32[]{:S(2)}, u32[]{:S(2)}) collective-permute-start(f32[16,512]{1,0:T(8,128)S(1)} %get-tuple-element.58), channel_id=1, source_target_pairs={{0,192},{16,208},{32,224},{48,240},{64,128},{80,144},{96,160},{112... | collective-permute-start | bytes 98312 | tf_op jit(solution)/shard_map/ppermute | solution.py:11
  82.5 2.8 %collective-permute-start.29 = (f32[16,512]{1,0:T(8,128)S(1)}, f32[16,512]{1,0:T(8,128)S(1)}, u32[]{:S(2)}, u32[]{:S(2)}) collective-permute-start(f32[16,512]{1,0:T(8,128)S(1)} %get-tuple-element.60), channel_id=1, source_target_pairs={{0,64},{16,80},{32,96},{48,112},{64,0},{80,16},{96,32},{112,48},{1... | collective-permute-start | bytes 98312 | tf_op jit(solution)/shard_map/ppermute | solution.py:11
  85.3 1.9 %multiply_convert_fusion.2 = bf16[512,1664]{1,0:T(8,128)(2,1)} fusion(bf16[256,4992]{1,0:T(8,128)(2,1)S(1)} %constant_dynamic-update-slice_fusion.13, bf16[256,1024]{1,0:T(8,128)(2,1)S(1)} %pad_maximum_fusion.5), kind=kOutput, calls=%fused_computation.2 | convolution fusion | flops 437911552 | bytes 2818048 | tf_op jit(solution)/shard_map/dot_general | solution.py:47
  (107 shorter events, 13.0 us)
Async XLA Ops:
  0.6 16.0 %copy-start = (bf16[512,1664]{1,0:T(8,128)(2,1)S(1)}, bf16[512,1664]{1,0:T(8,128)(2,1)}, u32[]{:S(2)}) copy-start(bf16[512,1664]{1,0:T(8,128)(2,1)} %param.6) | copy-start | bytes 5111812
  1.5 6.7 %collective-permute-start.2 = (bf16[16,1024]{1,0:T(8,128)(2,1)S(1)}, bf16[16,1024]{1,0:T(8,128)(2,1)S(1)}, u32[]{:S(2)}, u32[]{:S(2)}) collective-permute-start(bf16[16,1024]{1,0:T(8,128)(2,1)S(1)} %pad_add_fusion), channel_id=1, source_target_pairs={{0,192},{16,208},{32,224},{48,240},{64,128},{80,144},{96,160},{112... | collective-permute-start | bytes 98312 | tf_op jit(solution)/shard_map/ppermute | solution.py:11
  6.1 4.8 %collective-permute-start.1 = (bf16[16,1024]{1,0:T(8,128)(2,1)S(1)}, bf16[16,1024]{1,0:T(8,128)(2,1)S(1)}, u32[]{:S(2)}, u32[]{:S(2)}) collective-permute-start(bf16[16,1024]{1,0:T(8,128)(2,1)S(1)} %pad_add_fusion), channel_id=1, source_target_pairs={{0,128},{16,144},{32,160},{48,176},{64,192},{80,208},{96,224},{112... | collective-permute-start | bytes 98312 | tf_op jit(solution)/shard_map/ppermute | solution.py:11
  6.1 4.8 %collective-permute-start = (bf16[16,1024]{1,0:T(8,128)(2,1)S(1)}, bf16[16,1024]{1,0:T(8,128)(2,1)S(1)}, u32[]{:S(2)}, u32[]{:S(2)}) collective-permute-start(bf16[16,1024]{1,0:T(8,128)(2,1)S(1)} %pad_add_fusion), channel_id=1, source_target_pairs={{0,64},{16,80},{32,96},{48,112},{64,0},{80,16},{96,32},{112,48},{1... | collective-permute-start | bytes 98312 | tf_op jit(solution)/shard_map/ppermute | solution.py:11
  11.3 6.7 %collective-permute-start.6 = (bf16[64,1024]{1,0:T(8,128)(2,1)S(1)}, bf16[64,1024]{1,0:T(8,128)(2,1)S(1)}, u32[]{:S(2)}, u32[]{:S(2)}) collective-permute-start(bf16[64,1024]{1,0:T(8,128)(2,1)S(1)} %fusion.28), channel_id=1, source_target_pairs={{0,32},{16,48},{32,0},{48,16},{64,96},{80,112},{96,64},{112,80},{1... | collective-permute-start | bytes 393224 | tf_op jit(solution)/shard_map/ppermute | solution.py:11
  14.4 6.3 %collective-permute-start.5 = (bf16[64,1024]{1,0:T(8,128)(2,1)S(1)}, bf16[64,1024]{1,0:T(8,128)(2,1)S(1)}, u32[]{:S(2)}, u32[]{:S(2)}) collective-permute-start(bf16[64,1024]{1,0:T(8,128)(2,1)S(1)} %fusion.28), channel_id=1, source_target_pairs={{0,48},{16,32},{32,16},{48,0},{64,112},{80,96},{96,80},{112,64},{1... | collective-permute-start | bytes 393224 | tf_op jit(solution)/shard_map/ppermute | solution.py:11
  15.5 5.1 %collective-permute-start.4 = (bf16[64,1024]{1,0:T(8,128)(2,1)S(1)}, bf16[64,1024]{1,0:T(8,128)(2,1)S(1)}, u32[]{:S(2)}, u32[]{:S(2)}) collective-permute-start(bf16[64,1024]{1,0:T(8,128)(2,1)S(1)} %fusion.28), channel_id=1, source_target_pairs={{0,16},{16,0},{32,48},{48,32},{64,80},{80,64},{96,112},{112,96},{1... | collective-permute-start | bytes 393224 | tf_op jit(solution)/shard_map/ppermute | solution.py:11
  17.2 6.5 %collective-permute-start.3 = (f32[1,32,4992]{2,1,0:T(8,128)S(1)}, f32[1,32,4992]{2,1,0:T(8,128)S(1)}, u32[]{:S(2)}, u32[]{:S(2)}) collective-permute-start(f32[1,32,4992]{2,1,0:T(8,128)S(1)} %slice.261), channel_id=1, source_target_pairs={{0,1},{1,0},{2,3},{3,2},{4,5},{5,4},{6,7},{7,6},{8,9},{9,8},{10,11... | collective-permute-start | bytes 1916936 | tf_op jit(solution)/shard_map/ppermute | solution.py:11
  22.6 2.2 %collective-permute-start.7 = (f32[1,32,4992]{2,1,0:T(8,128)S(1)}, f32[1,32,4992]{2,1,0:T(8,128)S(1)}, u32[]{:S(2)}, u32[]{:S(2)}) collective-permute-start(f32[1,32,4992]{2,1,0:T(8,128)S(1)} %slice.265), channel_id=1, source_target_pairs={{0,1},{1,0},{2,3},{3,2},{4,5},{5,4},{6,7},{7,6},{8,9},{9,8},{10,11... | collective-permute-start | bytes 1916936 | tf_op jit(solution)/shard_map/ppermute | solution.py:11
  23.0 6.2 %collective-permute-start.11 = (f32[2,32,4992]{2,1,0:T(8,128)S(1)}, f32[2,32,4992]{2,1,0:T(8,128)S(1)}, u32[]{:S(2)}, u32[]{:S(2)}) collective-permute-start(f32[2,32,4992]{2,1,0:T(8,128)S(1)} %slice.272), channel_id=1, source_target_pairs={{0,1},{1,0},{2,3},{3,2},{4,5},{5,4},{6,7},{7,6},{8,9},{9,8},{10,11... | collective-permute-start | bytes 3833864 | tf_op jit(solution)/shard_map/ppermute | solution.py:11
  25.0 12.3 %collective-permute-start.10 = (bf16[2,8,4992]{2,1,0:T(8,128)(2,1)S(1)}, bf16[2,8,4992]{2,1,0:T(8,128)(2,1)S(1)}, u32[]{:S(2)}, u32[]{:S(2)}) collective-permute-start(bf16[2,8,4992]{2,1,0:T(8,128)(2,1)S(1)} %get-tuple-element.40), channel_id=1, source_target_pairs={{0,12},{1,13},{2,14},{3,15},{4,8},{5,9},{6,10},{7,11},{8,4},{9,5},... | collective-permute-start | bytes 479240 | tf_op jit(solution)/shard_map/ppermute | solution.py:11
  25.3 12.0 %collective-permute-start.9 = (bf16[2,8,4992]{2,1,0:T(8,128)(2,1)S(1)}, bf16[2,8,4992]{2,1,0:T(8,128)(2,1)S(1)}, u32[]{:S(2)}, u32[]{:S(2)}) collective-permute-start(bf16[2,8,4992]{2,1,0:T(8,128)(2,1)S(1)} %get-tuple-element.41), channel_id=1, source_target_pairs={{0,8},{1,9},{2,10},{3,11},{4,12},{5,13},{6,14},{7,15},{8,0},{9,1},... | collective-permute-start | bytes 479240 | tf_op jit(solution)/shard_map/ppermute | solution.py:11
  27.9 9.7 %collective-permute-start.8 = (bf16[2,8,4992]{2,1,0:T(8,128)(2,1)S(1)}, bf16[2,8,4992]{2,1,0:T(8,128)(2,1)S(1)}, u32[]{:S(2)}, u32[]{:S(2)}) collective-permute-start(bf16[2,8,4992]{2,1,0:T(8,128)(2,1)S(1)} %get-tuple-element.42), channel_id=1, source_target_pairs={{0,4},{1,5},{2,6},{3,7},{4,0},{5,1},{6,2},{7,3},{8,12},{9,13},{10,... | collective-permute-start | bytes 479240 | tf_op jit(solution)/shard_map/ppermute | solution.py:11
  29.4 13.3 %collective-permute-start.13 = (bf16[2,8,4992]{2,1,0:T(8,128)(2,1)S(1)}, bf16[2,8,4992]{2,1,0:T(8,128)(2,1)S(1)}, u32[]{:S(2)}, u32[]{:S(2)}) collective-permute-start(bf16[2,8,4992]{2,1,0:T(8,128)(2,1)S(1)} %get-tuple-element.43), channel_id=1, source_target_pairs={{0,12},{1,13},{2,14},{3,15},{4,8},{5,9},{6,10},{7,11},{8,4},{9,5},... | collective-permute-start | bytes 479240 | tf_op jit(solution)/shard_map/ppermute | solution.py:11
  29.7 13.0 %collective-permute-start.15 = (bf16[2,8,4992]{2,1,0:T(8,128)(2,1)S(1)}, bf16[2,8,4992]{2,1,0:T(8,128)(2,1)S(1)}, u32[]{:S(2)}, u32[]{:S(2)}) collective-permute-start(bf16[2,8,4992]{2,1,0:T(8,128)(2,1)S(1)} %get-tuple-element.44), channel_id=1, source_target_pairs={{0,8},{1,9},{2,10},{3,11},{4,12},{5,13},{6,14},{7,15},{8,0},{9,1},... | collective-permute-start | bytes 479240 | tf_op jit(solution)/shard_map/ppermute | solution.py:11
  37.3 6.1 %collective-permute-start.14 = (bf16[2,8,4992]{2,1,0:T(8,128)(2,1)S(1)}, bf16[2,8,4992]{2,1,0:T(8,128)(2,1)S(1)}, u32[]{:S(2)}, u32[]{:S(2)}) collective-permute-start(bf16[2,8,4992]{2,1,0:T(8,128)(2,1)S(1)} %get-tuple-element.45), channel_id=1, source_target_pairs={{0,4},{1,5},{2,6},{3,7},{4,0},{5,1},{6,2},{7,3},{8,12},{9,13},{10,... | collective-permute-start | bytes 479240 | tf_op jit(solution)/shard_map/ppermute | solution.py:11
  37.7 10.5 %collective-permute-start.12 = (bf16[2,8,4992]{2,1,0:T(8,128)(2,1)S(1)}, bf16[2,8,4992]{2,1,0:T(8,128)(2,1)S(1)}, u32[]{:S(2)}, u32[]{:S(2)}) collective-permute-start(bf16[2,8,4992]{2,1,0:T(8,128)(2,1)S(1)} %get-tuple-element.36), channel_id=1, source_target_pairs={{0,2},{1,3},{2,0},{3,1},{4,6},{5,7},{6,4},{7,5},{8,10},{9,11},{10,... | collective-permute-start | bytes 479240 | tf_op jit(solution)/shard_map/ppermute | solution.py:11
  43.5 14.2 %collective-permute-start.19 = (bf16[2,8,4992]{2,1,0:T(8,128)(2,1)S(1)}, bf16[2,8,4992]{2,1,0:T(8,128)(2,1)S(1)}, u32[]{:S(2)}, u32[]{:S(2)}) collective-permute-start(bf16[2,8,4992]{2,1,0:T(8,128)(2,1)S(1)} %fusion.41), channel_id=1, source_target_pairs={{0,2},{1,3},{2,0},{3,1},{4,6},{5,7},{6,4},{7,5},{8,10},{9,11},{10,... | collective-permute-start | bytes 479240 | tf_op jit(solution)/shard_map/ppermute | solution.py:11
  48.3 10.8 %collective-permute-start.18 = (bf16[2,8,4992]{2,1,0:T(8,128)(2,1)S(1)}, bf16[2,8,4992]{2,1,0:T(8,128)(2,1)S(1)}, u32[]{:S(2)}, u32[]{:S(2)}) collective-permute-start(bf16[2,8,4992]{2,1,0:T(8,128)(2,1)S(1)} %get-tuple-element.55), channel_id=1, source_target_pairs={{0,12},{1,13},{2,14},{3,15},{4,8},{5,9},{6,10},{7,11},{8,4},{9,5},... | collective-permute-start | bytes 479240 | tf_op jit(solution)/shard_map/ppermute | solution.py:11
  48.8 13.9 %collective-permute-start.17 = (bf16[2,8,4992]{2,1,0:T(8,128)(2,1)S(1)}, bf16[2,8,4992]{2,1,0:T(8,128)(2,1)S(1)}, u32[]{:S(2)}, u32[]{:S(2)}) collective-permute-start(bf16[2,8,4992]{2,1,0:T(8,128)(2,1)S(1)} %get-tuple-element.55), channel_id=1, source_target_pairs={{0,4},{1,5},{2,6},{3,7},{4,0},{5,1},{6,2},{7,3},{8,12},{9,13},{10,... | collective-permute-start | bytes 479240 | tf_op jit(solution)/shard_map/ppermute | solution.py:11
  50.2 12.5 %collective-permute-start.16 = (bf16[2,8,4992]{2,1,0:T(8,128)(2,1)S(1)}, bf16[2,8,4992]{2,1,0:T(8,128)(2,1)S(1)}, u32[]{:S(2)}, u32[]{:S(2)}) collective-permute-start(bf16[2,8,4992]{2,1,0:T(8,128)(2,1)S(1)} %get-tuple-element.55), channel_id=1, source_target_pairs={{0,8},{1,9},{2,10},{3,11},{4,12},{5,13},{6,14},{7,15},{8,0},{9,1},... | collective-permute-start | bytes 479240 | tf_op jit(solution)/shard_map/ppermute | solution.py:11
  57.9 8.3 %collective-permute-start.24 = (bf16[2,8,4992]{2,1,0:T(8,128)(2,1)S(1)}, bf16[2,8,4992]{2,1,0:T(8,128)(2,1)S(1)}, u32[]{:S(2)}, u32[]{:S(2)}) collective-permute-start(bf16[2,8,4992]{2,1,0:T(8,128)(2,1)S(1)} %get-tuple-element.56), channel_id=1, source_target_pairs={{0,12},{1,13},{2,14},{3,15},{4,8},{5,9},{6,10},{7,11},{8,4},{9,5},... | collective-permute-start | bytes 479240 | tf_op jit(solution)/shard_map/ppermute | solution.py:11
  58.3 7.9 %collective-permute-start.23 = (bf16[2,8,4992]{2,1,0:T(8,128)(2,1)S(1)}, bf16[2,8,4992]{2,1,0:T(8,128)(2,1)S(1)}, u32[]{:S(2)}, u32[]{:S(2)}) collective-permute-start(bf16[2,8,4992]{2,1,0:T(8,128)(2,1)S(1)} %get-tuple-element.56), channel_id=1, source_target_pairs={{0,4},{1,5},{2,6},{3,7},{4,0},{5,1},{6,2},{7,3},{8,12},{9,13},{10,... | collective-permute-start | bytes 479240 | tf_op jit(solution)/shard_map/ppermute | solution.py:11
  59.1 9.5 %collective-permute-start.22 = (bf16[2,8,4992]{2,1,0:T(8,128)(2,1)S(1)}, bf16[2,8,4992]{2,1,0:T(8,128)(2,1)S(1)}, u32[]{:S(2)}, u32[]{:S(2)}) collective-permute-start(bf16[2,8,4992]{2,1,0:T(8,128)(2,1)S(1)} %get-tuple-element.56), channel_id=1, source_target_pairs={{0,8},{1,9},{2,10},{3,11},{4,12},{5,13},{6,14},{7,15},{8,0},{9,1},... | collective-permute-start | bytes 479240 | tf_op jit(solution)/shard_map/ppermute | solution.py:11
  62.8 6.0 %collective-permute-start.20 = (bf16[2,32,4992]{2,1,0:T(8,128)(2,1)S(1)}, bf16[2,32,4992]{2,1,0:T(8,128)(2,1)S(1)}, u32[]{:S(2)}, u32[]{:S(2)}) collective-permute-start(bf16[2,32,4992]{2,1,0:T(8,128)(2,1)S(1)} %pad_maximum_fusion.3), channel_id=1, source_target_pairs={{0,1},{1,0},{2,3},{3,2},{4,5},{5,4},{6,7},{7,6},{8,9},{9,8},{10,11... | collective-permute-start | bytes 1916936 | tf_op jit(solution)/shard_map/ppermute | solution.py:11
  68.7 2.3 %collective-permute-start.25 = (bf16[2,32,4992]{2,1,0:T(8,128)(2,1)S(1)}, bf16[2,32,4992]{2,1,0:T(8,128)(2,1)S(1)}, u32[]{:S(2)}, u32[]{:S(2)}) collective-permute-start(bf16[2,32,4992]{2,1,0:T(8,128)(2,1)S(1)} %pad_maximum_fusion.4), channel_id=1, source_target_pairs={{0,1},{1,0},{2,3},{3,2},{4,5},{5,4},{6,7},{7,6},{8,9},{9,8},{10,11... | collective-permute-start | bytes 1916936 | tf_op jit(solution)/shard_map/ppermute | solution.py:11
  70.3 9.1 %collective-permute-start.21 = (f32[64,512]{1,0:T(8,128)S(1)}, f32[64,512]{1,0:T(8,128)S(1)}, u32[]{:S(2)}, u32[]{:S(2)}) collective-permute-start(f32[64,512]{1,0:T(8,128)S(1)} %slice.286), channel_id=1, source_target_pairs={{0,32},{16,48},{32,0},{48,16},{64,96},{80,112},{96,64},{112,80},{1... | collective-permute-start | bytes 393224 | tf_op jit(solution)/shard_map/ppermute | solution.py:11
  72.4 8.1 %collective-permute-start.26 = (f32[64,512]{1,0:T(8,128)S(1)}, f32[64,512]{1,0:T(8,128)S(1)}, u32[]{:S(2)}, u32[]{:S(2)}) collective-permute-start(f32[64,512]{1,0:T(8,128)S(1)} %get-tuple-element.52), channel_id=1, source_target_pairs={{0,48},{16,32},{32,16},{48,0},{64,112},{80,96},{96,80},{112,64},{1... | collective-permute-start | bytes 393224 | tf_op jit(solution)/shard_map/ppermute | solution.py:11
  74.2 6.4 %collective-permute-start.27 = (f32[64,512]{1,0:T(8,128)S(1)}, f32[64,512]{1,0:T(8,128)S(1)}, u32[]{:S(2)}, u32[]{:S(2)}) collective-permute-start(f32[64,512]{1,0:T(8,128)S(1)} %get-tuple-element.53), channel_id=1, source_target_pairs={{0,16},{16,0},{32,48},{48,32},{64,80},{80,64},{96,112},{112,96},{1... | collective-permute-start | bytes 393224 | tf_op jit(solution)/shard_map/ppermute | solution.py:11
  80.8 6.4 %collective-permute-start.28 = (f32[16,512]{1,0:T(8,128)S(1)}, f32[16,512]{1,0:T(8,128)S(1)}, u32[]{:S(2)}, u32[]{:S(2)}) collective-permute-start(f32[16,512]{1,0:T(8,128)S(1)} %get-tuple-element.58), channel_id=1, source_target_pairs={{0,192},{16,208},{32,224},{48,240},{64,128},{80,144},{96,160},{112... | collective-permute-start | bytes 98312 | tf_op jit(solution)/shard_map/ppermute | solution.py:11
  82.5 5.0 %collective-permute-start.30 = (f32[16,512]{1,0:T(8,128)S(1)}, f32[16,512]{1,0:T(8,128)S(1)}, u32[]{:S(2)}, u32[]{:S(2)}) collective-permute-start(f32[16,512]{1,0:T(8,128)S(1)} %get-tuple-element.59), channel_id=1, source_target_pairs={{0,128},{16,144},{32,160},{48,176},{64,192},{80,208},{96,224},{112... | collective-permute-start | bytes 98312 | tf_op jit(solution)/shard_map/ppermute | solution.py:11
  82.5 5.0 %collective-permute-start.29 = (f32[16,512]{1,0:T(8,128)S(1)}, f32[16,512]{1,0:T(8,128)S(1)}, u32[]{:S(2)}, u32[]{:S(2)}) collective-permute-start(f32[16,512]{1,0:T(8,128)S(1)} %get-tuple-element.60), channel_id=1, source_target_pairs={{0,64},{16,80},{32,96},{48,112},{64,0},{80,16},{96,32},{112,48},{1... | collective-permute-start | bytes 98312 | tf_op jit(solution)/shard_map/ppermute | solution.py:11
  (2 other events, 9.3 us)
